TPU v7x, 128 devices: a whole 4x4x4 slice. The times are simulated.
128 devices in a mesh: row: 8 (over x, core), col: 16 (over z, y).
Axes of the slice: x: 4, y: 4, z: 4, core: 2. Of those that a mesh axis runs over, the one named last changes fastest.
Arguments:
- panel: float32 [32768, 256], P(('row', 'col')), as said below
- trailing: float32 [32768, 4096], P('row', 'col'), may hold values from -6 to 6
- factors: bfloat16 [16384, 256, 128], P(('row', 'col')), may hold values from -1.1953125 to 1.1953125
- owner: int32 [16384, 1], P(('row', 'col')), may hold values from 0 to 127; in each aligned block of 128 rows (0 to 127, 128 to 255, ...) at most 2 rows name the same one
- tile_slot: int32 [16384], P(('row', 'col')), may hold values from 0 to 15
- ranks: int32 [16384], P(('row', 'col')), may hold values from 32 to 64
Outputs:
- updated: float32 [32768, 4096], P('row', 'col')
- lower: float32 [32768, 256], P(('row', 'col'))
Inputs may be any that keep to these rules, and one draw needn't show every extreme that they name: Within the rows of one device no owner is named more than 2 times, a bound that some block reaches. `panel`: rows 0 to 255 form a symmetric positive definite block.
All inputs are finite; a program needn't handle non-finite values.
Results may differ from a plain program's by a relative error of at most 0.0003.
Values may be sent and summed in bfloat16 or wider, within the bound.
No kernel may reach another device: no remote copies, remote signals or barrier semaphores. Data moves between devices by JAX's collectives and lax.ppermute only.
A program may use at most 192 MiB of HBM per device.

v0:
```python
import jax
import jax.numpy as jnp
from jax import lax
from jax.sharding import PartitionSpec as P


def broadcast(shard, axis, root):
    mine = lax.axis_index(axis) == root
    return lax.psum(jnp.where(mine, shard, jnp.zeros_like(shard)), axis)


def shards(panel, trailing, factors, owner, tile_slot, ranks):
    rows_devs = lax.axis_size("row")
    cols_devs = lax.axis_size("col")
    devices = rows_devs * cols_devs
    items = factors.shape[0]
    tile = panel.shape[0]
    width_two = factors.shape[2]
    rank_max = width_two // 2
    slots_per = max(2, (3 * items + 2 * devices - 1) // (2 * devices))
    total = devices * slots_per
    dest = owner[:, 0]
    match = (dest[:, None] == jnp.arange(devices)[None, :]).astype(jnp.int32)
    position = jnp.sum((jnp.cumsum(match, axis=0) - match) * match, axis=1)
    target = dest * slots_per + position
    col_index = jnp.arange(width_two)
    keep = (col_index[None, :] >= rank_max) | (col_index[None, :] < ranks[:, None])
    masked = jnp.where(keep[:, None, :], factors, jnp.zeros_like(factors))
    outbox = jnp.zeros((total, tile, width_two), jnp.bfloat16).at[target].set(masked)
    labels = jnp.full((total,), -1, jnp.int32).at[target].set(tile_slot)
    inbox, tags = (
        lax.all_to_all(
            outbox.reshape(devices, slots_per, tile, width_two),
            ("row", "col"),
            split_axis=0,
            concat_axis=0,
            tiled=True,
        ),
        lax.all_to_all(
            labels.reshape(devices, slots_per),
            ("row", "col"),
            split_axis=0,
            concat_axis=0,
            tiled=True,
        ),
    )
    inbox = inbox.reshape(16, total // 16, tile, width_two)
    tags = tags.reshape(16, total // 16)
    tile_ids = jnp.arange(cols_devs)

    def absorb(accum, block):
        pieces, marks = block
        dense = jnp.einsum(
            "sak,sbk->sab",
            pieces[..., :rank_max],
            pieces[..., rank_max:],
            preferred_element_type=jnp.float32,
        )
        onehot = (tile_ids[:, None] == marks[None, :]).astype(jnp.float32)
        added = jnp.dot(
            onehot, dense.reshape(marks.shape[0], tile * tile), precision=lax.Precision.HIGHEST
        )
        return (accum + added, None)

    accum, _ = lax.scan(absorb, jnp.zeros((cols_devs, tile * tile), jnp.float32), (inbox, tags))
    extend = accum.reshape(cols_devs * tile, tile)
    factor = jnp.linalg.cholesky(panel)
    inverse = lax.linalg.triangular_solve(
        factor, jnp.eye(tile, dtype=jnp.float32), left_side=True, lower=True
    )
    shared_inverse = broadcast(inverse, ("row", "col"), 0)
    lower = jnp.dot(panel, shared_inverse.T, precision=lax.Precision.HIGHEST)
    columns = broadcast(lower, "row", 1)
    update = jnp.dot(
        lax.all_gather(lower, "col", axis=0, tiled=True), columns.T, precision=lax.Precision.HIGHEST
    )
    updated = trailing + extend - update
    return (updated, lower)


def solution(mesh):
    return jax.shard_map(
        shards,
        mesh=mesh,
        in_specs=(
            P(("row", "col"), None),
            P("row", "col"),
            P(("row", "col"), None, None),
            P(("row", "col"), None),
            P(("row", "col")),
            P(("row", "col")),
        ),
        out_specs=(P("row", "col"), P(("row", "col"), None)),
        check_vma=False,
    )
```

profile of v0, /device:TPU:102, one launch (start us, length us, event | category | flops | bytes accessed | tf_op | source)
XLA Modules:
  0.0 652.2 jit_solution(360181046423496470)
XLA Ops:
  11.5 9.8 %all-to-all-start = ((s32[128,1,2]{2,1,0:T(1,128)}), s32[128,1,2]{2,1,0:T(1,128)S(1)}, u32[]{:S(2)}, u32[]{:S(2)}) async-start(s32[128,1,2]{2,1,0:T(1,128)} %bitcast.3), calls=%async_computation | async-start | bytes 131072 | tf_op jit(solution)/shard_map/all_to_all | solution.py:39
  35.5 23.4 %scatter_fusion = bf16[256,256,128]{2,1,0:T(8,128)(2,1)} fusion(bf16[256,256,128]{2,1,0:T(8,128)(2,1)} %broadcast_in_dim.21, s32[128]{0:T(128)S(1)} %fusion.16, bf16[128,256,128]{2,1,0:T(8,128)(2,1)} %broadcast_select_fusion), kind=kCustom, calls=%fused_computation.1 | custom fusion | bytes 25166336 | tf_op jit(solution)/shard_map/scatter | solution.py:29
  59.0 10.2 %all-to-all-start.1 = ((bf16[128,2,256,128]{3,2,1,0:T(8,128)(2,1)}), bf16[128,2,256,128]{3,2,1,0:T(8,128)(2,1)}, u32[]{:S(2)}, u32[]{:S(2)}) async-start(bf16[128,2,256,128]{3,2,1,0:T(8,128)(2,1)} %bitcast.66), calls=%async_computation.1 | async-start | bytes 33554432 | tf_op jit(solution)/shard_map/all_to_all | solution.py:32
  69.6 11.7 %cholesky.50 = f32[128,128]{1,0:T(8,128)S(1)} custom-call(f32[128,128]{1,0:T(8,128)S(1)} %cholesky.118), custom_call_target="Cholesky" | custom-call | tf_op jit(solution)/shard_map/jit(cholesky)/cholesky | solution.py:67
  81.4 9.8 %custom-call.14 = f32[1,128,128]{1,2,0:T(8,128)S(1)} custom-call(f32[1,128,128]{2,1,0:T(8,128)S(1)} %get-tuple-element.76), custom_call_target="InvertDiagBlocksLowerTriangular" | custom-call | tf_op jit(solution)/shard_map/jit(cholesky)/cholesky | solution.py:67
  91.7 11.7 %cholesky.105 = f32[128,128]{1,0:T(8,128)S(1)} custom-call(f32[128,128]{1,0:T(8,128)S(1)} %convolution_subtract_fusion.2), custom_call_target="Cholesky" | custom-call | tf_op jit(solution)/shard_map/jit(cholesky)/cholesky | solution.py:67
  109.8 19.7 %custom-call.15 = f32[2,128,128]{1,2,0:T(8,128)S(1)} custom-call(f32[2,128,128]{2,1,0:T(8,128)S(1)} %get-tuple-element.37), custom_call_target="InvertDiagBlocksLowerTriangular" | custom-call | tf_op jit(solution)/shard_map/triangular_solve | solution.py:68
  131.2 248.1 %all-reduce.4.cloned.1.call-done = f32[256,256]{1,0:T(8,128)} async-done(((f32[256,256]{1,0:T(8,128)}), f32[256,256]{1,0:T(8,128)}) %all-reduce.4.cloned.1.call-update) | async-done | bytes 262160 | tf_op jit(solution)/shard_map/psum | solution.py:9
  383.1 22.4 %copy.14 = bf16[128,2,256,128]{2,3,1,0:T(8,128)(2,1)} copy(bf16[128,2,256,128]{3,2,1,0:T(8,128)(2,1)} %all-to-all-done.1) | data formatting | bytes 33554432 | tf_op jit(solution)/shard_map/all_to_all | solution.py:32
  405.5 226.1 %while.13 = (s32[]{:T(128)}, f32[16,65536]{1,0:T(8,128)}, s32[16,16]{1,0:T(8,128)S(1)}, bf16[16,16,256,128]{2,3,1,0:T(8,128)(2,1)}, s32[]{:T(128)}, /*index=5*/s32[]{:T(128)}) while((s32[]{:T(128)}, f32[16,65536]{1,0:T(8,128)}, s32[16,16]{1,0:T(8,128)S(1)}, bf16[16,16,256,128]{2,3,1,0:T(8,128)(2,1)}, s32[]{:T(128)}, ...), condition=%wide.region_5.6_spmd.clone, body=%wide.region_4.5_spmd.clone.sunk | while | flops 337641728 | bytes 28311832 | solution.py:65
  424.9 7.8 %convolution_add_fusion.2 = f32[16,65536]{1,0:T(8,128)} fusion(f32[16,65536]{1,0:T(8,128)} %bitcast.64, f32[16,65536]{1,0:T(8,128)} %get-tuple-element.159, pred[]{:T(512)S(6)} %compare.26, s32[16]{0:T(128)S(1)} %dynamic-slice_bitcast_fusion.5), kind=kOutput, calls=%fused_computation.5.clone.1 | convolution fusion | flops 203424000 | bytes 12582977 | tf_op jit(solution)/shard_map/while/body/eval_jaxpr/dot_general | solution.py:60
  439.1 7.8 %convolution_add_fusion.2 = f32[16,65536]{1,0:T(8,128)} fusion(f32[16,65536]{1,0:T(8,128)} %bitcast.64, f32[16,65536]{1,0:T(8,128)} %get-tuple-element.159, pred[]{:T(512)S(6)} %compare.26, s32[16]{0:T(128)S(1)} %dynamic-slice_bitcast_fusion.5), kind=kOutput, calls=%fused_computation.5.clone.1 | convolution fusion | flops 203424000 | bytes 12582977 | tf_op jit(solution)/shard_map/while/body/eval_jaxpr/dot_general | solution.py:60
  453.3 7.8 %convolution_add_fusion.2 = f32[16,65536]{1,0:T(8,128)} fusion(f32[16,65536]{1,0:T(8,128)} %bitcast.64, f32[16,65536]{1,0:T(8,128)} %get-tuple-element.159, pred[]{:T(512)S(6)} %compare.26, s32[16]{0:T(128)S(1)} %dynamic-slice_bitcast_fusion.5), kind=kOutput, calls=%fused_computation.5.clone.1 | convolution fusion | flops 203424000 | bytes 12582977 | tf_op jit(solution)/shard_map/while/body/eval_jaxpr/dot_general | solution.py:60
  467.6 7.8 %convolution_add_fusion.2 = f32[16,65536]{1,0:T(8,128)} fusion(f32[16,65536]{1,0:T(8,128)} %bitcast.64, f32[16,65536]{1,0:T(8,128)} %get-tuple-element.159, pred[]{:T(512)S(6)} %compare.26, s32[16]{0:T(128)S(1)} %dynamic-slice_bitcast_fusion.5), kind=kOutput, calls=%fused_computation.5.clone.1 | convolution fusion | flops 203424000 | bytes 12582977 | tf_op jit(solution)/shard_map/while/body/eval_jaxpr/dot_general | solution.py:60
  481.8 7.9 %convolution_add_fusion.2 = f32[16,65536]{1,0:T(8,128)} fusion(f32[16,65536]{1,0:T(8,128)} %bitcast.64, f32[16,65536]{1,0:T(8,128)} %get-tuple-element.159, pred[]{:T(512)S(6)} %compare.26, s32[16]{0:T(128)S(1)} %dynamic-slice_bitcast_fusion.5), kind=kOutput, calls=%fused_computation.5.clone.1 | convolution fusion | flops 203424000 | bytes 12582977 | tf_op jit(solution)/shard_map/while/body/eval_jaxpr/dot_general | solution.py:60
  496.2 7.8 %convolution_add_fusion.2 = f32[16,65536]{1,0:T(8,128)} fusion(f32[16,65536]{1,0:T(8,128)} %bitcast.64, f32[16,65536]{1,0:T(8,128)} %get-tuple-element.159, pred[]{:T(512)S(6)} %compare.26, s32[16]{0:T(128)S(1)} %dynamic-slice_bitcast_fusion.5), kind=kOutput, calls=%fused_computation.5.clone.1 | convolution fusion | flops 203424000 | bytes 12582977 | tf_op jit(solution)/shard_map/while/body/eval_jaxpr/dot_general | solution.py:60
  510.4 7.8 %convolution_add_fusion.2 = f32[16,65536]{1,0:T(8,128)} fusion(f32[16,65536]{1,0:T(8,128)} %bitcast.64, f32[16,65536]{1,0:T(8,128)} %get-tuple-element.159, pred[]{:T(512)S(6)} %compare.26, s32[16]{0:T(128)S(1)} %dynamic-slice_bitcast_fusion.5), kind=kOutput, calls=%fused_computation.5.clone.1 | convolution fusion | flops 203424000 | bytes 12582977 | tf_op jit(solution)/shard_map/while/body/eval_jaxpr/dot_general | solution.py:60
  524.6 7.8 %convolution_add_fusion.2 = f32[16,65536]{1,0:T(8,128)} fusion(f32[16,65536]{1,0:T(8,128)} %bitcast.64, f32[16,65536]{1,0:T(8,128)} %get-tuple-element.159, pred[]{:T(512)S(6)} %compare.26, s32[16]{0:T(128)S(1)} %dynamic-slice_bitcast_fusion.5), kind=kOutput, calls=%fused_computation.5.clone.1 | convolution fusion | flops 203424000 | bytes 12582977 | tf_op jit(solution)/shard_map/while/body/eval_jaxpr/dot_general | solution.py:60
  538.8 7.8 %convolution_add_fusion.2 = f32[16,65536]{1,0:T(8,128)} fusion(f32[16,65536]{1,0:T(8,128)} %bitcast.64, f32[16,65536]{1,0:T(8,128)} %get-tuple-element.159, pred[]{:T(512)S(6)} %compare.26, s32[16]{0:T(128)S(1)} %dynamic-slice_bitcast_fusion.5), kind=kOutput, calls=%fused_computation.5.clone.1 | convolution fusion | flops 203424000 | bytes 12582977 | tf_op jit(solution)/shard_map/while/body/eval_jaxpr/dot_general | solution.py:60
  552.9 7.8 %convolution_add_fusion.2 = f32[16,65536]{1,0:T(8,128)} fusion(f32[16,65536]{1,0:T(8,128)} %bitcast.64, f32[16,65536]{1,0:T(8,128)} %get-tuple-element.159, pred[]{:T(512)S(6)} %compare.26, s32[16]{0:T(128)S(1)} %dynamic-slice_bitcast_fusion.5), kind=kOutput, calls=%fused_computation.5.clone.1 | convolution fusion | flops 203424000 | bytes 12582977 | tf_op jit(solution)/shard_map/while/body/eval_jaxpr/dot_general | solution.py:60
  567.1 7.8 %convolution_add_fusion.2 = f32[16,65536]{1,0:T(8,128)} fusion(f32[16,65536]{1,0:T(8,128)} %bitcast.64, f32[16,65536]{1,0:T(8,128)} %get-tuple-element.159, pred[]{:T(512)S(6)} %compare.26, s32[16]{0:T(128)S(1)} %dynamic-slice_bitcast_fusion.5), kind=kOutput, calls=%fused_computation.5.clone.1 | convolution fusion | flops 203424000 | bytes 12582977 | tf_op jit(solution)/shard_map/while/body/eval_jaxpr/dot_general | solution.py:60
  581.3 7.8 %convolution_add_fusion.2 = f32[16,65536]{1,0:T(8,128)} fusion(f32[16,65536]{1,0:T(8,128)} %bitcast.64, f32[16,65536]{1,0:T(8,128)} %get-tuple-element.159, pred[]{:T(512)S(6)} %compare.26, s32[16]{0:T(128)S(1)} %dynamic-slice_bitcast_fusion.5), kind=kOutput, calls=%fused_computation.5.clone.1 | convolution fusion | flops 203424000 | bytes 12582977 | tf_op jit(solution)/shard_map/while/body/eval_jaxpr/dot_general | solution.py:60
  623.9 7.8 %convolution_add_fusion.2 = f32[16,65536]{1,0:T(8,128)} fusion(f32[16,65536]{1,0:T(8,128)} %bitcast.64, f32[16,65536]{1,0:T(8,128)} %get-tuple-element.159, pred[]{:T(512)S(6)} %compare.26, s32[16]{0:T(128)S(1)} %dynamic-slice_bitcast_fusion.5), kind=kOutput, calls=%fused_computation.5.clone.1 | convolution fusion | flops 203424000 | bytes 12582977 | tf_op jit(solution)/shard_map/while/body/eval_jaxpr/dot_general | solution.py:60
  635.5 10.2 %convolution_subtract_fusion = f32[4096,256]{1,0:T(8,128)} fusion(f32[4096,256]{1,0:T(8,128)} %all-gather.2.cloned.1.call-done, f32[256,256]{1,0:T(8,128)} %all-reduce.6.cloned.1.call-done, f32[4096,256]{1,0:T(8,128)} %param.9, f32[4096,256]{1,0:T(8,128)} %reshape.80), kind=kOutput, calls=%fused_computation.14 | convolution fusion | flops 3223322624 | bytes 17039360 | tf_op jit(solution)/shard_map/dot_general | solution.py:74
  (120 shorter events, 162.5 us)
Async XLA Ops:
  11.5 47.5 %all-to-all-start = ((s32[128,1,2]{2,1,0:T(1,128)}), s32[128,1,2]{2,1,0:T(1,128)S(1)}, u32[]{:S(2)}, u32[]{:S(2)}) async-start(s32[128,1,2]{2,1,0:T(1,128)} %bitcast.3), calls=%async_computation | async-start | bytes 131072 | tf_op jit(solution)/shard_map/all_to_all | solution.py:39
  59.0 10.5 %copy-start = (f32[256,256]{1,0:T(8,128)S(1)}, f32[256,256]{1,0:T(8,128)}, u32[]{:S(2)}) copy-start(f32[256,256]{1,0:T(8,128)} %param.8) | copy-start | bytes 786436
  59.0 324.1 %all-to-all-start.1 = ((bf16[128,2,256,128]{3,2,1,0:T(8,128)(2,1)}), bf16[128,2,256,128]{3,2,1,0:T(8,128)(2,1)}, u32[]{:S(2)}, u32[]{:S(2)}) async-start(bf16[128,2,256,128]{3,2,1,0:T(8,128)(2,1)} %bitcast.66), calls=%async_computation.1 | async-start | bytes 33554432 | tf_op jit(solution)/shard_map/all_to_all | solution.py:32
  69.2 310.1 %all-reduce.4.cloned.1.call-start = ((), (), s32[]{:S(2)}) async-start(), calls=%async_computation.2 | async-start | bytes 524288 | tf_op jit(solution)/shard_map/psum | solution.py:9
  131.2 504.3 %all-reduce.6.cloned.1.call-start = ((), (), s32[]{:S(2)}) async-start(), calls=%async_computation.4 | async-start | bytes 524288 | tf_op jit(solution)/shard_map/psum | solution.py:9
  381.5 254.0 %all-gather.2.cloned.1.call-start = ((), (), s32[]{:S(2)}) async-start(), calls=%async_computation.3 | async-start | bytes 4456448 | tf_op jit(solution)/shard_map/all_gather | solution.py:75
Sparse Core Ops, SparseCore 0:
  131.3 247.9 all-reduce.3
  381.6 57.2 all-reduce.5
  441.9 52.7 all-gather.1
where the time goes:
time: 658 us; the launch traced here: 652 us
  waiting for transfers between devices  248 us (38%)
  local copies, waits for them, and re-layouts  154 us (23%)
  matrix products  149 us (23%)
  other arithmetic  65.7 us (10%)
  starting transfers between devices  20.3 us (3%)
  between operations  15.3 us (2%)
    psum x2, waiting for transfers between devices, broadcast(): return lax.psum(jnp.where(mine, shard, jnp.zeros_like(shard)), axis)  248 us
    dot_general x16, matrix products, absorb(): jnp.dot(onehot, dense.reshape(marks.shape[0], tile * tile), precision=lax...  123 us
    while x16, local copies, waits for them, and re-layouts  69.7 us
    another operation x6, other arithmetic, shards(): factor = jnp.linalg.cholesky(panel)  34 us
    scatter x1, local copies, waits for them, and re-layouts, shards(): jnp.zeros((total, tile, width_two), jnp.bfloat16).at[target].set(masked)  23.4 us
    all_to_all x1, local copies, waits for them, and re-layouts, shards(): lax.all_to_all(outbox.reshape(devices, slots_per, tile, width_two), ('row...  22.4 us
    squeeze x16, local copies, waits for them, and re-layouts, shards(): lax.scan(absorb, jnp.zeros((cols_devs, tile * tile), jnp.float32), (inbox...  21 us
    another operation x3, other arithmetic, shards(): lax.linalg.triangular_solve(factor, jnp.eye(tile, dtype=jnp.float32), lef...  19.7 us
  transfers between devices with their start and end apart: 5, of which 1 were waited for; matrix products, arithmetic and copies ran while one was open for 54% of the time, Pallas kernels for 0%

commit v1 on v0

v1 whole, which is shorter than its diff:
```python
import jax
import jax.numpy as jnp
from jax import lax
from jax.experimental import pallas as pl
from jax.experimental.pallas import tpu as pltpu
from jax.sharding import PartitionSpec as P

ALL = ("row", "col")
HIGHEST = lax.Precision.HIGHEST
VMEM_LIMIT = 48 * 1024 * 1024


def pack(target, factors, devices):
    items, rows, width = factors.shape
    chunk = 16

    def kernel(target_ref, factors_ref, first_ref, second_ref, held, load_sems, store_sems):
        def load(c):
            part = pl.ds(c * chunk, chunk)
            return pltpu.make_async_copy(factors_ref.at[part], held.at[part], load_sems.at[c])

        @pl.loop(0, items // chunk)
        def _(c):
            load(c).start()

        @pl.loop(0, items // chunk)
        def _(c):
            load(c).wait()

            @pl.loop(0, chunk)
            def _(i):
                k = c * chunk + i
                place = target_ref[k]

                @pl.when(place < devices)
                def _():
                    pltpu.make_async_copy(held.at[k], first_ref.at[place], store_sems.at[k]).start()

                @pl.when(place >= devices)
                def _():
                    pltpu.make_async_copy(held.at[k], second_ref.at[place - devices], store_sems.at[k]).start()

        @pl.loop(0, items)
        def _(k):
            pltpu.make_async_copy(held.at[k], first_ref.at[0], store_sems.at[k]).wait()

    box = jax.ShapeDtypeStruct((devices, rows, width), factors.dtype)
    size = items * rows * width * 2
    return pl.pallas_call(
        kernel,
        out_shape=(box, box),
        grid_spec=pltpu.PrefetchScalarGridSpec(
            num_scalar_prefetch=1,
            grid=(1,),
            in_specs=[pl.BlockSpec(memory_space=pl.ANY)],
            out_specs=[pl.BlockSpec(memory_space=pl.ANY)] * 2,
            scratch_shapes=[
                pltpu.VMEM((items, rows, width), factors.dtype),
                pltpu.SemaphoreType.DMA((items // chunk,)),
                pltpu.SemaphoreType.DMA((items,)),
            ],
        ),
        compiler_params=pltpu.CompilerParams(vmem_limit_bytes=VMEM_LIMIT),
        cost_estimate=pl.CostEstimate(flops=0, bytes_accessed=2 * size, transcendentals=0),
        name="pack",
    )(target, factors)


def absorb(tags, inbox, base, tiles):
    slots, rows, width = inbox.shape
    half = width // 2
    chunk = 16

    def kernel(tags_ref, inbox_ref, base_ref, out_ref):
        step = pl.program_id(0)

        @pl.when(step == 0)
        def _():
            out_ref[...] = base_ref[...]

        lane = lax.broadcasted_iota(jnp.int32, (rows, half), 1)

        @pl.loop(0, chunk)
        def _(i):
            tag = tags_ref[step * chunk + i]

            @pl.when(tag >= 0)
            def _():
                slot = tag // 64
                rank = tag % 64 + 1
                left = jnp.where(lane < rank, inbox_ref[i, :, :half], jnp.bfloat16(0))
                right = inbox_ref[i, :, half:]
                out_ref[slot] += lax.dot_general(
                    left, right, (((1,), (1,)), ((), ())), preferred_element_type=jnp.float32
                )

    whole = pl.BlockSpec((tiles, rows, rows), lambda s, t: (0, 0, 0))
    return pl.pallas_call(
        kernel,
        out_shape=jax.ShapeDtypeStruct((tiles, rows, rows), jnp.float32),
        grid_spec=pltpu.PrefetchScalarGridSpec(
            num_scalar_prefetch=1,
            grid=(slots // chunk,),
            in_specs=[pl.BlockSpec((chunk, rows, width), lambda s, t: (s, 0, 0)), whole],
            out_specs=whole,
        ),
        compiler_params=pltpu.CompilerParams(vmem_limit_bytes=VMEM_LIMIT),
        cost_estimate=pl.CostEstimate(
            flops=2 * slots * rows * rows * half,
            bytes_accessed=slots * rows * width * 2 + 8 * tiles * rows * rows,
            transcendentals=0,
        ),
        name="absorb",
    )(tags, inbox, base)


def shards(panel, trailing, factors, owner, tile_slot, ranks):
    rows_devs = lax.axis_size("row")
    cols_devs = lax.axis_size("col")
    devices = rows_devs * cols_devs
    items = factors.shape[0]
    tile = panel.shape[0]
    me = lax.axis_index("row") * cols_devs + lax.axis_index("col")

    dest = owner[:, 0]
    order = jnp.arange(items)
    earlier = (dest[:, None] == dest[None, :]) & (order[:, None] > order[None, :])
    target = dest + devices * jnp.any(earlier, axis=1).astype(jnp.int32)
    first_out, second_out = pack(target, factors, devices)

    def spread(value, steps):
        for pairs in steps:
            value = value + sum([lax.ppermute(value, ALL, p) for p in pairs])
        return value

    along_x = [[(0, r * cols_devs)] for r in range(2, rows_devs, 2)]
    evens = [r * cols_devs for r in range(0, rows_devs, 2)]
    along_y = [[(e, e + y) for e in evens] for y in range(1, 4)]
    along_z = [[(e + y, e + y + z) for e in evens for y in range(4)] for z in range(4, cols_devs, 4)]
    across = [[(e + c, e + c + cols_devs) for e in evens for c in range(cols_devs)]]
    diagonal = spread(
        jnp.where(me == 0, panel, jnp.zeros_like(panel)), [along_x, along_y, along_z, across]
    )

    code = ((dest * 16 + tile_slot) * 64 + ranks - 1).astype(jnp.float32)
    label = jnp.zeros((8, tile), jnp.float32).at[0, :items].set(code)
    by_row = lax.all_gather(jnp.concatenate([panel, label]), "row", axis=0).reshape(rows_devs, tile + 8, tile)
    columns_panel = by_row[1, :tile]
    by_col = lax.all_gather(jnp.concatenate([panel, by_row[:, tile]]), "col", axis=0)
    front = by_col[:, :tile].reshape(cols_devs * tile, tile)
    codes = by_col[:, tile:, :items].transpose(1, 0, 2).reshape(devices, items).astype(jnp.int32)
    mine = codes // 1024 == me
    place = jnp.arange(items)[None, :]
    first = jnp.min(jnp.where(mine, place, items), axis=1)
    last = jnp.max(jnp.where(mine, place, -1), axis=1)
    first_tags = jnp.max(jnp.where(mine & (place == first[:, None]), codes % 1024, -1), axis=1)
    second_tags = jnp.max(
        jnp.where(mine & (place == last[:, None]) & (first < last)[:, None], codes % 1024, -1), axis=1
    )

    factor = jnp.linalg.cholesky(diagonal)
    inverse = lax.linalg.triangular_solve(
        factor, jnp.eye(tile, dtype=jnp.float32), left_side=True, lower=True
    )
    lower = jnp.dot(panel, inverse.T, precision=HIGHEST)
    columns = jnp.dot(columns_panel, inverse.T, precision=HIGHEST)
    weights = jnp.dot(inverse.T, columns.T, precision=HIGHEST)
    base = trailing - jnp.dot(front, weights, precision=HIGHEST)

    first_in = lax.all_to_all(first_out, ALL, split_axis=0, concat_axis=0, tiled=True)
    second_in = lax.all_to_all(second_out, ALL, split_axis=0, concat_axis=0, tiled=True)
    total = absorb(first_tags, first_in, base.reshape(cols_devs, tile, tile), cols_devs)
    total = absorb(second_tags, second_in, total, cols_devs)
    return (total.reshape(cols_devs * tile, tile), lower)


def solution(mesh):
    return jax.shard_map(
        shards,
        mesh=mesh,
        in_specs=(
            P(ALL, None),
            P("row", "col"),
            P(ALL, None, None),
            P(ALL, None),
            P(ALL),
            P(ALL),
        ),
        out_specs=(P("row", "col"), P(ALL, None)),
        check_vma=False,
    )
```

time: 658 us -> 442 us (0.67)
  the two profiles are of different devices: /device:TPU:102 before, /device:TPU:95 now
where the time goes in v1:
time: 442 us; the launch traced here: 434 us
  waiting for transfers between devices  212 us (48%)
  Pallas kernels  84 us (19%)
  other arithmetic  60.1 us (14%)
  starting transfers between devices  33.3 us (8%)
  local copies, waits for them, and re-layouts  15.9 us (4%)
  between operations  15.9 us (4%)
  matrix products  12.6 us (3%)
    ppermute x10, waiting for transfers between devices, spread(): value = value + sum([lax.ppermute(value, ALL, p) for p in pairs])  112 us
    pallas_call x2, Pallas kernels, absorb(): pl.pallas_call(kernel, out_shape=jax.ShapeDtypeStruct((tiles, rows, rows)...  76 us
    all_to_all x1, waiting for transfers between devices, shards(): lax.all_to_all(first_out, ALL, split_axis=0, concat_axis=0, tiled=True)  57.6 us
    all_gather x1, waiting for transfers between devices, shards(): lax.all_gather(jnp.concatenate([panel, label]), 'row', axis=0)  42.6 us
    another operation x6, other arithmetic, shards(): factor = jnp.linalg.cholesky(diagonal)  34 us
    another operation x3, other arithmetic, shards(): lax.linalg.triangular_solve(factor, jnp.eye(tile, dtype=jnp.float32), lef...  19.7 us
    all_to_all x1, starting transfers between devices, shards(): lax.all_to_all(second_out, ALL, split_axis=0, concat_axis=0, tiled=True)  15 us
    all_to_all x1, starting transfers between devices, shards(): lax.all_to_all(first_out, ALL, split_axis=0, concat_axis=0, tiled=True)  10.6 us
  transfers between devices with their start and end apart: 14, of which 3 were waited for; matrix products, arithmetic and copies ran while one was open for 19% of the time, Pallas kernels for 9%

profile of v1, /device:TPU:95, one launch (start us, length us, event | category | flops | bytes accessed | tf_op | source)
XLA Modules:
  0.0 434.4 jit_solution(5942812711570158376)
XLA Ops:
  7.2 0.9 fusion.16
  8.8 8.1 %pack.1 = (bf16[128,256,128]{2,1,0:T(8,128)(2,1)}, bf16[128,256,128]{2,1,0:T(8,128)(2,1)}) custom-call(s32[128]{0:T(128)S(1)} %get-tuple-element.68.target_ref, bf16[128,256,128]{2,1,0:T(8,128)(2,1)} %factors_ref.1), custom_call_target="tpu_custom_call" | custom-call | bytes 16777216 | tf_op jit(solution)/shard_map/pack/pallas_call | solution.py:49
  16.9 10.6 %all-to-all-start.1 = ((bf16[128,256,128]{2,1,0:T(8,128)(2,1)}), bf16[128,256,128]{2,1,0:T(8,128)(2,1)}, u32[]{:S(2)}, u32[]{:S(2)}) async-start(bf16[128,256,128]{2,1,0:T(8,128)(2,1)} %get-tuple-element.17), calls=%async_computation.1 | async-start | bytes 16777216 | tf_op jit(solution)/shard_map/all_to_all | solution.py:170
  28.4 42.6 %all-gather.5.cloned.1.call-done = f32[2112,256]{1,0:T(8,128)} async-done(((f32[264,256]{1,0:T(8,128)}), f32[2112,256]{1,0:T(8,128)}) %all-gather.5.cloned.1.call-update) | async-done | bytes 2162704 | tf_op jit(solution)/shard_map/all_gather | solution.py:147
  72.5 57.6 %all-to-all-done.1.inbox_ref = bf16[128,256,128]{2,1,0:T(8,128)(2,1)} async-done(((bf16[128,256,128]{2,1,0:T(8,128)(2,1)}), bf16[128,256,128]{2,1,0:T(8,128)(2,1)}, u32[]{:S(2)}, u32[]{:S(2)}) %all-to-all-start.1) | async-done | bytes 8388640 | tf_op jit(solution)/shard_map/all_to_all | solution.py:170
  130.1 15.0 %all-to-all-start = ((bf16[128,256,128]{2,1,0:T(8,128)(2,1)}), bf16[128,256,128]{2,1,0:T(8,128)(2,1)}, u32[]{:S(2)}, u32[]{:S(2)}) async-start(bf16[128,256,128]{2,1,0:T(8,128)(2,1)} %get-tuple-element.16), calls=%async_computation | async-start | bytes 16777216 | tf_op jit(solution)/shard_map/all_to_all | solution.py:171
  151.8 1.5 collective-permute-start.9
  153.3 112.1 %collective-permute-done.9 = f32[256,256]{0,1:T(8,128)S(1)} collective-permute-done((f32[256,256]{0,1:T(8,128)S(1)}, f32[256,256]{0,1:T(8,128)S(1)}, u32[]{:S(2)}, u32[]{:S(2)}) %collective-permute-start.9) | collective-permute-done | bytes 262176 | tf_op jit(solution)/shard_map/ppermute | solution.py:133
  265.7 11.7 %cholesky.49 = f32[128,128]{1,0:T(8,128)S(1)} custom-call(f32[128,128]{1,0:T(8,128)S(1)} %cholesky.115), custom_call_target="Cholesky" | custom-call | tf_op jit(solution)/shard_map/jit(cholesky)/cholesky | solution.py:161
  277.5 9.8 %custom-call.14 = f32[1,128,128]{1,2,0:T(8,128)S(1)} custom-call(f32[1,128,128]{2,1,0:T(8,128)S(1)} %get-tuple-element.67), custom_call_target="InvertDiagBlocksLowerTriangular" | custom-call | tf_op jit(solution)/shard_map/jit(cholesky)/cholesky | solution.py:161
  287.9 11.7 %cholesky.103 = f32[128,128]{1,0:T(8,128)S(1)} custom-call(f32[128,128]{1,0:T(8,128)S(1)} %slice_subtract_fusion), custom_call_target="Cholesky" | custom-call | tf_op jit(solution)/shard_map/jit(cholesky)/cholesky | solution.py:161
  302.1 4.7 %while.2 = (s32[]{:T(128)}, f32[256,256]{0,1:T(8,128)S(1)}, s32[2,2]{1,0:T(2,128)S(1)}, f32[2,128,128]{2,1,0:T(8,128)S(1)}, s32[]{:T(128)}) while((s32[]{:T(128)}, f32[256,256]{0,1:T(8,128)S(1)}, s32[2,2]{1,0:T(2,128)S(1)}, f32[2,128,128]{2,1,0:T(8,128)S(1)}, s32[]{:T(128)}) %tuple.42), condition=%wide.while_cond.1, body=%wide.while_body.1.sunk | while | flops 2 | bytes 393329 | solution.py:162
  302.9 1.5 dynamic-slice.14
  305.2 1.5 dynamic-slice.14
  306.8 19.7 %custom-call.15 = f32[2,128,128]{1,2,0:T(8,128)S(1)} custom-call(f32[2,128,128]{2,1,0:T(8,128)S(1)} %get-tuple-element.25), custom_call_target="InvertDiagBlocksLowerTriangular" | custom-call | tf_op jit(solution)/shard_map/triangular_solve | solution.py:162
  328.6 1.4 fusion
  330.6 4.6 %slice.88 = f32[16,256,256]{2,1,0:T(8,128)} slice(f32[16,264,256]{2,1,0:T(8,128)} %bitcast.73), slice={[0:16], [0:256], [0:256]} | slice | bytes 8388608 | tf_op jit(solution)/shard_map/slice | solution.py:150
  335.2 1.5 select_reduce_fusion.4
  336.7 1.5 select_reduce_fusion.2
  338.6 8.8 %convolution_subtract_fusion = f32[4096,256]{1,0:T(8,128)} fusion(f32[4096,256]{1,0:T(8,128)} %param.9, f32[4096,256]{1,0:T(8,128)} %bitcast.72, f32[256,256]{1,0:T(8,128)S(1)} %fusion.2), kind=kOutput, calls=%fused_computation.2 | convolution fusion | flops 3222274048 | bytes 12845056 | tf_op jit(solution)/shard_map/dot_general | solution.py:168
  347.4 37.6 %absorb.2.base_ref = f32[16,256,256]{2,1,0:T(8,128)S(1)} custom-call(s32[128]{0:T(128)S(1)} %reduce_max.35.tags_ref, bf16[128,256,128]{2,1,0:T(8,128)(2,1)} %all-to-all-done.1.inbox_ref, f32[16,256,256]{2,1,0:T(8,128)} %bitcast.71), custom_call_target="tpu_custom_call" | custom-call | flops 1073741824 | bytes 16777216 | tf_op jit(solution)/shard_map/absorb/pallas_call | solution.py:98
  385.0 2.0 copy-done
  387.1 2.2 copy-done.1
  389.2 38.3 %absorb.3 = f32[16,256,256]{2,1,0:T(8,128)} custom-call(s32[128]{0:T(128)S(1)} %reduce_max.33.tags_ref, bf16[128,256,128]{2,1,0:T(8,128)(2,1)} %all-to-all-done.inbox_ref, f32[16,256,256]{2,1,0:T(8,128)S(1)} %copy-done.1), custom_call_target="tpu_custom_call" | custom-call | flops 1073741824 | bytes 16777216 | tf_op jit(solution)/shard_map/absorb/pallas_call | solution.py:98
  (77 shorter events, 16.1 us)
Async XLA Ops:
  16.8 10.7 %copy-start.2 = (f32[256,256]{1,0:T(8,128)S(1)}, f32[256,256]{1,0:T(8,128)}, u32[]{:S(2)}) copy-start(f32[256,256]{1,0:T(8,128)} %param.8) | copy-start | bytes 786436
  16.9 113.2 %all-to-all-start.1 = ((bf16[128,256,128]{2,1,0:T(8,128)(2,1)}), bf16[128,256,128]{2,1,0:T(8,128)(2,1)}, u32[]{:S(2)}, u32[]{:S(2)}) async-start(bf16[128,256,128]{2,1,0:T(8,128)(2,1)} %get-tuple-element.17), calls=%async_computation.1 | async-start | bytes 16777216 | tf_op jit(solution)/shard_map/all_to_all | solution.py:170
  27.5 43.4 %all-gather.5.cloned.1.call-start = ((), (), s32[]{:S(2)}) async-start(), calls=%async_computation.2 | async-start | bytes 2433024 | tf_op jit(solution)/shard_map/all_gather | solution.py:147
  28.3 302.3 %all-gather.7.cloned.1.call-start = ((), (), s32[]{:S(2)}) async-start(), calls=%async_computation.3 | async-start | bytes 4595712 | tf_op jit(solution)/shard_map/all_gather | solution.py:149
  130.1 257.0 %all-to-all-start = ((bf16[128,256,128]{2,1,0:T(8,128)(2,1)}), bf16[128,256,128]{2,1,0:T(8,128)(2,1)}, u32[]{:S(2)}, u32[]{:S(2)}) async-start(bf16[128,256,128]{2,1,0:T(8,128)(2,1)} %get-tuple-element.16), calls=%async_computation | async-start | bytes 16777216 | tf_op jit(solution)/shard_map/all_to_all | solution.py:171
  145.3 2.1 collective-permute-start.2
  146.0 1.4 collective-permute-start.1
  146.6 0.7 collective-permute-start
  147.4 2.1 collective-permute-start.5
  148.1 1.4 collective-permute-start.4
  148.8 0.7 collective-permute-start.3
  149.6 2.1 collective-permute-start.8
  150.3 1.4 collective-permute-start.7
  151.0 0.7 collective-permute-start.6
  151.8 113.7 %collective-permute-start.9 = (f32[256,256]{0,1:T(8,128)S(1)}, f32[256,256]{0,1:T(8,128)S(1)}, u32[]{:S(2)}, u32[]{:S(2)}) collective-permute-start(f32[256,256]{0,1:T(8,128)S(1)} %add_add_fusion), channel_id=1, source_target_pairs={{0,16},{1,17},{2,18},{3,19},{4,20},{5,21},{6,22},{7,23},{8,24},{9,... | collective-permute-start | bytes 786440 | tf_op jit(solution)/shard_map/ppermute | solution.py:133
  385.0 2.0 copy-start
  387.1 2.2 copy-start.1
Sparse Core Ops, SparseCore 0:
  30.6 40.2 all-gather.4
  73.6 178.7 all-gather.6

commit v2 on v1

v2 whole, which is shorter than its diff:
```python
import jax
import jax.numpy as jnp
from jax import lax
from jax.experimental import pallas as pl
from jax.experimental.pallas import tpu as pltpu
from jax.sharding import Mesh
from jax.sharding import PartitionSpec as P

ALL = ("x", "core", "z", "y")
ROW = ("x", "core")
COL = ("z", "y")
GROUP = 4
UNROLL = 4
SCHEDULED_FLOPS = 2 * 10**11
HIGHEST = lax.Precision.HIGHEST
PACK_VMEM = 58 * 1024 * 1024
ABSORB_VMEM = 58 * 1024 * 1024


def pack(target, labels, factors, devices):
    items, rows, width = factors.shape
    extra = labels.shape[1]
    chunk = 16

    def kernel(target_ref, labels_ref, factors_ref, first_ref, second_ref, held, load_sems, store_sems, label_sem):
        def load(c):
            part = pl.ds(c * chunk, chunk)
            return pltpu.make_async_copy(factors_ref.at[part], held.at[part], load_sems.at[c])

        def to_first(k, place):
            return pltpu.make_async_copy(held.at[k], first_ref.at[place, pl.ds(0, rows)], store_sems.at[k])

        def to_second(k, place):
            return pltpu.make_async_copy(held.at[k], second_ref.at[place], store_sems.at[k])

        @pl.loop(0, items // chunk)
        def _(c):
            load(c).start()

        tail = pltpu.make_async_copy(labels_ref, first_ref.at[:, pl.ds(rows, extra)], label_sem)
        tail.start()

        @pl.loop(0, items // chunk)
        def _(c):
            load(c).wait()

            @pl.loop(0, chunk)
            def _(i):
                k = c * chunk + i
                place = target_ref[k]

                @pl.when(place < devices)
                def _():
                    to_first(k, place).start()

                @pl.when(place >= devices)
                def _():
                    to_second(k, place - devices).start()

        tail.wait()

        @pl.loop(0, items)
        def _(k):
            to_second(k, 0).wait()

    size = items * rows * width * 2
    hbm = pl.BlockSpec(memory_space=pltpu.HBM)
    return pl.pallas_call(
        kernel,
        out_shape=(
            pltpu.HBM((devices, rows + extra, width), factors.dtype),
            pltpu.HBM((devices, rows, width), factors.dtype),
        ),
        in_specs=[pl.BlockSpec(memory_space=pltpu.SMEM), pl.BlockSpec(memory_space=pltpu.VMEM), hbm],
        out_specs=[hbm] * 2,
        scratch_shapes=[
            pltpu.VMEM((items, rows, width), factors.dtype),
            pltpu.SemaphoreType.DMA((items // chunk,)),
            pltpu.SemaphoreType.DMA((items,)),
            pltpu.SemaphoreType.DMA,
        ],
        compiler_params=pltpu.CompilerParams(vmem_limit_bytes=PACK_VMEM),
        cost_estimate=pl.CostEstimate(flops=0, bytes_accessed=2 * size, transcendentals=0),
        name="pack",
    )(target, labels, factors)


def plan(tags, tiles):
    slots = tags.shape[0]
    groups = slots // GROUP + tiles + UNROLL
    tile_of = jnp.where(tags >= 0, tags // 64, -1)
    order, tile = jnp.arange(slots), jnp.arange(tiles)
    before = jnp.sum((tile_of[:, None] == tile_of[None, :]) & (order[:, None] > order[None, :]), axis=1)
    need = (jnp.sum(tile_of[None, :] == tile[:, None], axis=1) + GROUP - 1) // GROUP
    end = jnp.sum(jnp.where(tile[None, :] <= tile[:, None], need[None, :], 0), axis=1)
    start = jnp.sum(jnp.where(tile_of[:, None] == tile[None, :], (end - need)[None, :], 0), axis=1)
    place = jnp.where(tags >= 0, start * GROUP + before, -1)
    entry = jnp.max(
        jnp.where(
            place[None, :] == jnp.arange(groups * GROUP)[:, None],
            (order * 128 + tags % 64 + 1)[None, :],
            -1,
        ),
        axis=1,
    )
    group_tile = jnp.sum((jnp.arange(groups)[:, None] >= end[None, :]).astype(jnp.int32), axis=1)
    return entry, jnp.minimum(group_tile, tiles - 1), end[tiles - 1 :]


def absorb(tags, inbox, base, update=()):
    slots, _, width = inbox.shape
    tiles, rows, _ = base.shape
    half = width // 2
    quarter = tiles // 4

    def kernel(entry_ref, tile_ref, count_ref, inbox_ref, base_ref, *refs):
        if update:
            front_ref, weights_ref, out_ref, held, total, sems, front = refs
        else:
            out_ref, held, total, sems = refs
        lane = lax.broadcasted_iota(jnp.int32, (16, width), 1)

        def load(q, kind):
            part = pl.ds(q * quarter, quarter)
            if kind:
                return pltpu.make_async_copy(front_ref.at[part], front.at[part], sems.at[4 + q])
            return pltpu.make_async_copy(base_ref.at[part], total.at[part], sems.at[q])

        for q in range(4):
            load(q, 0).start()
            if update:
                load(q, 1).start()
        items = pltpu.make_async_copy(inbox_ref.at[:, pl.ds(0, rows)], held, sems.at[8])
        items.start()

        for q in range(4):
            load(q, 0).wait()
            if update:
                load(q, 1).wait()

                @pl.loop(0, quarter // 2)
                def _(t):
                    pair = pl.ds(q * quarter + 2 * t, 2)
                    product = jnp.dot(
                        front[pair].reshape(2 * rows, rows),
                        weights_ref[...],
                        precision=HIGHEST,
                        preferred_element_type=jnp.float32,
                    )
                    total[pair] -= product.reshape(2, rows, rows)

        items.wait()

        def product(group):
            first = entry_ref[GROUP * group]
            first = jnp.where(first >= 0, first, entry_ref[0])

            def item(j):
                entry = entry_ref[GROUP * group + j]
                entry = jnp.where(entry >= 0, entry, (first // 128) * 128)
                return held[entry // 128], entry % 128

            left, right = [], []
            for j in range(0, GROUP, 2):
                (one, one_rank), (two, two_rank) = item(j), item(j + 1)
                keep = (lane < one_rank) | ((lane >= half) & (lane < half + two_rank))
                us = jnp.concatenate([one[:, :half], two[:, :half]], axis=1)
                us = us.reshape(rows // 16, 16, width) * keep.astype(us.dtype)[None]
                left.append(us.reshape(rows, width))
                right.append(jnp.concatenate([one[:, half:], two[:, half:]], axis=1))
            return lax.dot_general(
                jnp.concatenate(left, axis=1),
                jnp.concatenate(right, axis=1),
                (((1,), (1,)), ((), ())),
                preferred_element_type=jnp.float32,
            )

        @pl.loop(0, (count_ref[0] + UNROLL - 1) // UNROLL)
        def _(step):
            products = [product(step * UNROLL + u) for u in range(UNROLL)]
            for u in range(UNROLL):
                total[tile_ref[step * UNROLL + u]] += products[u]

        result = pltpu.make_async_copy(total, out_ref, sems.at[9])
        result.start()
        result.wait()

    smem, vmem = pl.BlockSpec(memory_space=pltpu.SMEM), pl.BlockSpec(memory_space=pltpu.VMEM)
    hbm = pl.BlockSpec(memory_space=pltpu.HBM)
    tiled = pltpu.VMEM(base.shape, base.dtype)
    return pl.pallas_call(
        kernel,
        out_shape=pltpu.HBM(base.shape, base.dtype),
        in_specs=[smem] * 3 + [hbm] * 2 + [hbm, vmem][: len(update)],
        out_specs=hbm,
        scratch_shapes=[pltpu.VMEM((slots, rows, width), inbox.dtype), tiled, pltpu.SemaphoreType.DMA((10,))]
        + [tiled][: len(update)],
        compiler_params=pltpu.CompilerParams(vmem_limit_bytes=ABSORB_VMEM),
        cost_estimate=pl.CostEstimate(
            flops=2 * slots * rows * rows * half,
            bytes_accessed=slots * rows * width * 2 + 8 * tiles * rows * rows,
            transcendentals=0,
        ),
        name="absorb",
    )(*plan(tags, tiles), inbox, base, *update)


def hold(array):
    def kernel(array_ref, out_ref):
        pass

    hbm = pl.BlockSpec(memory_space=pltpu.HBM)
    return pl.pallas_call(
        kernel,
        out_shape=pltpu.HBM(array.shape, array.dtype),
        in_specs=[hbm],
        out_specs=hbm,
        input_output_aliases={0: 0},
        cost_estimate=pl.CostEstimate(flops=SCHEDULED_FLOPS, bytes_accessed=0, transcendentals=0),
        name="hold",
    )(array)


def inverse_factor(block):
    half = block.shape[0] // 2
    eye = jnp.eye(half, dtype=block.dtype)

    def invert(part):
        factor = jnp.linalg.cholesky(part)
        return lax.linalg.triangular_solve(factor, eye, left_side=True, lower=True)

    first = invert(block[:half, :half])
    cross = 0.5 * (block[half:, :half] + block[:half, half:].T)
    below = jnp.dot(cross, first.T, precision=HIGHEST)
    second = invert(block[half:, half:] - jnp.dot(below, below.T, precision=HIGHEST))
    corner = -jnp.dot(second, jnp.dot(below, first, precision=HIGHEST), precision=HIGHEST)
    return jnp.concatenate(
        [jnp.concatenate([first, jnp.zeros_like(first)], axis=1), jnp.concatenate([corner, second], axis=1)]
    )


def shards(panel, trailing, factors, owner, tile_slot, ranks):
    rows_devs = lax.axis_size(ROW)
    cols_devs = lax.axis_size(COL)
    devices = rows_devs * cols_devs
    items = factors.shape[0]
    tile = panel.shape[0]
    me = lax.axis_index(ALL)

    dest = owner[:, 0]
    order = jnp.arange(items)
    same = dest[:, None] == dest[None, :]
    second = jnp.any(same & (order[:, None] > order[None, :]), axis=1)
    target = dest + devices * second.astype(jnp.int32)

    lands = target[None, :] == jnp.arange(2 * devices)[:, None]
    facts = jnp.stack([tile_slot, ranks])
    facts = jnp.max(jnp.where(lands[None], facts[:, None, :], 0), axis=2).reshape(2, 2, devices)
    facts = facts.transpose(2, 1, 0).reshape(devices, 1, 4).astype(factors.dtype)
    labels = jnp.pad(facts, ((0, 0), (0, 15), (0, factors.shape[2] - 4)))
    first_out, second_out = pack(target, labels, factors, devices)

    def spread(value, steps):
        return sum([lax.ppermute(value, ALL, pairs) for pairs in steps])

    def number(x, core, z, y):
        return ((x * 2 + core) * 4 + z) * 4 + y

    four = range(4)
    x, core = lax.axis_index("x"), lax.axis_index("core")

    front = lax.all_gather(panel, COL, axis=0, tiled=True)

    first_hop = [
        [(0, number(0, 0, 0, d))] + [(number(0, 1, z, y), number(d, 1, z, y)) for z in four for y in four]
        for d in (1, 2, 3)
    ]
    along_z = [[(number(0, 0, 0, y), number(0, 0, z, y)) for y in four] for z in (1, 2, 3)]
    along_x = [[(number(0, 0, z, y), number(x, 0, z, y)) for z in four for y in four] for x in (1, 2, 3)]
    swap = [[(number(x, c, z, y), number(x, 1 - c, z, y)) for x in four for c in (0, 1) for z in four for y in four]]
    held = jnp.where((me == 0) | ((x == 0) & (core == 1)), panel, spread(panel, first_hop))
    held, first_out, second_out = lax.optimization_barrier((held, first_out, second_out))
    for steps in (along_z, along_x):
        held = held + spread(held, steps)
    other = spread(held, swap)
    diagonal, columns_panel = jnp.where(core == 0, held, other), jnp.where(core == 0, other, held)

    diagonal, columns_panel, first_out = lax.optimization_barrier((diagonal, columns_panel, first_out))
    first_in = lax.all_to_all(first_out, ALL, split_axis=0, concat_axis=0, tiled=True)

    inverse = inverse_factor(diagonal)
    inverse, second_out = lax.optimization_barrier((inverse, second_out))
    second_in = lax.all_to_all(second_out, ALL, split_axis=0, concat_axis=0, tiled=True)

    facts = first_in[:, tile, :4].astype(jnp.int32)
    first_tags, second_tags = [facts[:, 2 * i] * 64 + facts[:, 2 * i + 1] - 1 for i in (0, 1)]

    lower = jnp.dot(panel, inverse.T, precision=HIGHEST)
    columns = jnp.dot(columns_panel, inverse.T, precision=HIGHEST)
    weights = jnp.dot(inverse.T, columns.T, precision=HIGHEST)
    tiled = (cols_devs, tile, tile)
    total = absorb(first_tags, first_in, trailing.reshape(tiled))
    front, total = lax.optimization_barrier((front.reshape(tiled), total))
    total = absorb(second_tags, second_in, total, (hold(front), weights))
    return (total.reshape(cols_devs * tile, tile), lower)


def solution(mesh):
    fine = Mesh(mesh.devices.reshape(4, 2, 4, 4), ALL)
    return jax.shard_map(
        shards,
        mesh=fine,
        in_specs=(
            P(ALL, None),
            P(ROW, COL),
            P(ALL, None, None),
            P(ALL, None),
            P(ALL),
            P(ALL),
        ),
        out_specs=(P(ROW, COL), P(ALL, None)),
        check_vma=False,
    )
```

time: 442 us -> 311 us (0.70)
  the two profiles are of different devices: /device:TPU:95 before, /device:TPU:102 now
where the time goes in v2:
time: 311 us
  waiting for transfers between devices  170 us (55%)
  other arithmetic  54.5 us (18%)
  Pallas kernels  36.8 us (12%)
  starting transfers between devices  25.1 us (8%)
  between operations  14.5 us (5%)
  local copies, waits for them, and re-layouts  5.78 us (2%)
  matrix products  3.88 us (1%)
    all_gather x1, waiting for transfers between devices, shards(): front = lax.all_gather(panel, COL, axis=0, tiled=True)  76 us
    all_to_all x1, waiting for transfers between devices, shards(): lax.all_to_all(first_out, ALL, split_axis=0, concat_axis=0, tiled=True)  61 us
    pallas_call x2, Pallas kernels, absorb(): pl.pallas_call(kernel, out_shape=pltpu.HBM(base.shape, base.dtype), in_sp...  28.1 us
    another operation x6, other arithmetic, invert(): factor = jnp.linalg.cholesky(part)  24.8 us
    another operation x4, other arithmetic, invert(): return lax.linalg.triangular_solve(factor, eye, left_side=True, lower=True)  21.1 us
    ppermute x10, waiting for transfers between devices, spread(): return sum([lax.ppermute(value, ALL, pairs) for pairs in steps])  18 us
    all_to_all x1, waiting for transfers between devices, shards(): lax.all_to_all(second_out, ALL, split_axis=0, concat_axis=0, tiled=True)  14.7 us
    all_to_all x1, starting transfers between devices, shards(): lax.all_to_all(first_out, ALL, split_axis=0, concat_axis=0, tiled=True)  9.27 us
  transfers between devices with their start and end apart: 13, of which 5 were waited for; matrix products, arithmetic and copies ran while one was open for 20% of the time, Pallas kernels for 7%

profile of v2, /device:TPU:102, one launch (start us, length us, event | category | flops | bytes accessed | tf_op | source)
XLA Modules:
  0.0 310.8 jit_solution(18439777937672561090)
XLA Ops:
  7.2 1.1 copy.36
  10.3 0.9 fusion.26
  11.9 0.7 pad_add_fusion
  13.0 0.9 pad.5.labels_ref
  13.9 8.8 %pack.1 = (bf16[128,272,128]{2,1,0:T(8,128)(2,1)}, bf16[128,256,128]{2,1,0:T(8,128)(2,1)}) custom-call(s32[128]{0:T(128)} %copy-done.1, bf16[128,16,128]{2,1,0:T(8,128)(2,1)} %pad.5.labels_ref, bf16[128,256,128]{2,1,0:T(8,128)(2,1)} %factors_ref.1), custom_call_target="tpu_custom_call" | custom-call | bytes 16777216 | tf_op jit(solution)/shard_map/pack/pallas_call | solution.py:68
  26.3 1.3 collective-permute-start.8
  27.6 16.5 %collective-permute-done.8 = f32[256,256]{0,1:T(8,128)S(1)} collective-permute-done((f32[256,256]{0,1:T(8,128)S(1)}, f32[256,256]{0,1:T(8,128)S(1)}, u32[]{:S(2)}, u32[]{:S(2)}) %collective-permute-start.8) | collective-permute-done | bytes 262176 | tf_op jit(solution)/shard_map/ppermute | solution.py:264
  44.2 1.5 collective-permute-done.9
  45.8 9.3 %all-to-all-start = ((bf16[128,272,128]{2,1,0:T(8,128)(2,1)}), bf16[128,272,128]{2,1,0:T(8,128)(2,1)}, u32[]{:S(2)}, u32[]{:S(2)}) async-start(bf16[128,272,128]{2,1,0:T(8,128)(2,1)} %get-tuple-element.20), calls=%async_computation | async-start | bytes 17825792 | tf_op jit(solution)/shard_map/all_to_all | solution.py:289
  56.1 11.7 %cholesky.44 = f32[128,128]{1,0:T(8,128)S(1)} custom-call(f32[128,128]{1,0:T(8,128)S(1)} %fusion.21), custom_call_target="Cholesky" | custom-call | tf_op jit(solution)/shard_map/jit(cholesky)/cholesky | solution.py:229
  69.1 9.8 %custom-call.6 = f32[1,128,128]{1,2,0:T(8,128)S(1)} custom-call(f32[1,128,128]{2,1,0:T(8,128)S(1)} %fusion.4), custom_call_target="InvertDiagBlocksLowerTriangular" | custom-call | tf_op jit(solution)/shard_map/triangular_solve/custom-call.0 | solution.py:230
  79.9 11.7 %cholesky.55 = f32[128,128]{1,0:T(8,128)S(1)} custom-call(f32[128,128]{1,0:T(8,128)S(1)} %fusion.18), custom_call_target="Cholesky" | custom-call | tf_op jit(solution)/shard_map/jit(cholesky)/cholesky | solution.py:229
  93.0 10.0 %custom-call.7 = f32[1,128,128]{1,2,0:T(8,128)S(1)} custom-call(f32[1,128,128]{2,1,0:T(8,128)S(1)} %fusion.5), custom_call_target="InvertDiagBlocksLowerTriangular" | custom-call | tf_op jit(solution)/shard_map/triangular_solve/custom-call.0 | solution.py:230
  104.3 0.8 copy.45
  105.7 1.3 fusion.39.refs_1_
  107.0 61.0 %all-to-all-done.inbox_ref = bf16[128,272,128]{2,1,0:T(8,128)(2,1)} async-done(((bf16[128,272,128]{2,1,0:T(8,128)(2,1)}), bf16[128,272,128]{2,1,0:T(8,128)(2,1)}, u32[]{:S(2)}, u32[]{:S(2)}) %all-to-all-start) | async-done | bytes 8912928 | tf_op jit(solution)/shard_map/all_to_all | solution.py:289
  168.0 8.8 %all-to-all-start.1 = ((bf16[128,256,128]{2,1,0:T(8,128)(2,1)}), bf16[128,256,128]{2,1,0:T(8,128)(2,1)}, u32[]{:S(2)}, u32[]{:S(2)}) async-start(bf16[128,256,128]{2,1,0:T(8,128)(2,1)} %get-tuple-element.23), calls=%async_computation.1 | async-start | bytes 16777216 | tf_op jit(solution)/shard_map/all_to_all | solution.py:293
  176.8 1.0 slice_convert_fusion
  180.6 0.7 convert_reduce_fusion
  182.6 13.1 %absorb.2.base_ref = f32[16,256,256]{2,1,0:T(8,128)} custom-call(s32[208]{0:T(256)} %select_reduce_fusion.1.entry_ref, s32[52]{0:T(128)} %broadcast_minimum_fusion.tile_ref, s32[1]{0:T(128)} %slice.49.count_ref, bf16[128,272,128]{2,1,0:T(8,128)(2,1)} %all-to-all-done.inbox_ref, f32[16,256,256]{2,1,0:T(8,128)} %bitcast.48), custom_call_target="tpu_custom_call" | custom-call | flops 1073741824 | bytes 16777216 | tf_op jit(solution)/shard_map/absorb/pallas_call | solution.py:191
  195.7 76.0 %all-gather.2.cloned.1.call-done = f32[4096,256]{1,0:T(8,128)} async-done(((f32[256,256]{1,0:T(8,128)}), f32[4096,256]{1,0:T(8,128)}) %all-gather.2.cloned.1.call-update) | async-done | bytes 4194320 | tf_op jit(solution)/shard_map/all_gather | solution.py:272
  273.1 0.7 select_reduce_fusion.2.entry_ref
  274.3 14.7 %all-to-all-done.1.inbox_ref = bf16[128,256,128]{2,1,0:T(8,128)(2,1)} async-done(((bf16[128,256,128]{2,1,0:T(8,128)(2,1)}), bf16[128,256,128]{2,1,0:T(8,128)(2,1)}, u32[]{:S(2)}, u32[]{:S(2)}) %all-to-all-start.1) | async-done | bytes 8388640 | tf_op jit(solution)/shard_map/all_to_all | solution.py:293
  289.0 14.9 %absorb.3 = f32[16,256,256]{2,1,0:T(8,128)} custom-call(s32[208]{0:T(256)} %select_reduce_fusion.2.entry_ref, s32[52]{0:T(128)} %broadcast_minimum_fusion.1.tile_ref, s32[1]{0:T(128)} %slice.42.count_ref, bf16[128,256,128]{2,1,0:T(8,128)(2,1)} %all-to-all-done.1.inbox_ref, f32[16,256,256]{2,1,0:T(8,128)} %absorb.2.base_ref, f32[16,256,256]{2,1,0:T(8,128)} %hold.1.refs_0_, ...), custom_call_target="tpu_custom_call" | custom-call | flops 1073741824 | bytes 16777216 | tf_op jit(solution)/shard_map/absorb/pallas_call | solution.py:191
  (90 shorter events, 19.0 us)
Async XLA Ops:
  8.2 14.4 %collective-permute-start = (f32[256,256]{0,1:T(8,128)S(1)}, f32[256,256]{0,1:T(8,128)S(1)}, u32[]{:S(2)}, u32[]{:S(2)}) collective-permute-start(f32[256,256]{0,1:T(8,128)S(1)} %copy.36), channel_id=1, source_target_pairs={{0,1},{16,48},{17,49},{18,50},{19,51},{20,52},{21,53},{22,54},{23,... | collective-permute-start | bytes 786440 | tf_op jit(solution)/shard_map/ppermute | solution.py:264
  8.9 13.7 %collective-permute-start.1 = (f32[256,256]{0,1:T(8,128)S(1)}, f32[256,256]{0,1:T(8,128)S(1)}, u32[]{:S(2)}, u32[]{:S(2)}) collective-permute-start(f32[256,256]{0,1:T(8,128)S(1)} %copy.36), channel_id=1, source_target_pairs={{0,2},{16,80},{17,81},{18,82},{19,83},{20,84},{21,85},{22,86},{23,... | collective-permute-start | bytes 786440 | tf_op jit(solution)/shard_map/ppermute | solution.py:264
  9.6 13.0 %collective-permute-start.2 = (f32[256,256]{0,1:T(8,128)S(1)}, f32[256,256]{0,1:T(8,128)S(1)}, u32[]{:S(2)}, u32[]{:S(2)}) collective-permute-start(f32[256,256]{0,1:T(8,128)S(1)} %copy.36), channel_id=1, source_target_pairs={{0,3},{16,112},{17,113},{18,114},{19,115},{20,116},{21,117},{22,11... | collective-permute-start | bytes 786440 | tf_op jit(solution)/shard_map/ppermute | solution.py:264
  11.9 2.0 copy-start.1
  22.7 2.1 collective-permute-start.3
  23.4 1.4 collective-permute-start.4
  24.1 0.7 collective-permute-start.5
  24.9 2.7 collective-permute-start.6
  25.6 2.0 collective-permute-start.7
  26.3 17.8 %collective-permute-start.8 = (f32[256,256]{0,1:T(8,128)S(1)}, f32[256,256]{0,1:T(8,128)S(1)}, u32[]{:S(2)}, u32[]{:S(2)}) collective-permute-start(f32[256,256]{0,1:T(8,128)S(1)} %add_add_fusion.1), channel_id=1, source_target_pairs={{0,96},{1,97},{2,98},{3,99},{4,100},{5,101},{6,102},{7,103},{8,104... | collective-permute-start | bytes 786440 | tf_op jit(solution)/shard_map/ppermute | solution.py:264
  44.1 1.6 collective-permute-start.9
  45.8 58.1 %copy-start = (f32[256,256]{1,0:T(8,128)S(1)}, f32[256,256]{1,0:T(8,128)}, u32[]{:S(2)}) copy-start(f32[256,256]{1,0:T(8,128)} %param.9) | copy-start | bytes 786436
  45.8 122.2 %all-to-all-start = ((bf16[128,272,128]{2,1,0:T(8,128)(2,1)}), bf16[128,272,128]{2,1,0:T(8,128)(2,1)}, u32[]{:S(2)}, u32[]{:S(2)}) async-start(bf16[128,272,128]{2,1,0:T(8,128)(2,1)} %get-tuple-element.20), calls=%async_computation | async-start | bytes 17825792 | tf_op jit(solution)/shard_map/all_to_all | solution.py:289
  55.1 216.6 %all-gather.2.cloned.1.call-start = ((), (), s32[]{:S(2)}) async-start(), calls=%async_computation.2 | async-start | bytes 4456448 | tf_op jit(solution)/shard_map/all_gather | solution.py:272
  168.0 121.0 %all-to-all-start.1 = ((bf16[128,256,128]{2,1,0:T(8,128)(2,1)}), bf16[128,256,128]{2,1,0:T(8,128)(2,1)}, u32[]{:S(2)}, u32[]{:S(2)}) async-start(bf16[128,256,128]{2,1,0:T(8,128)(2,1)} %get-tuple-element.23), calls=%async_computation.1 | async-start | bytes 16777216 | tf_op jit(solution)/shard_map/all_to_all | solution.py:293
  178.1 3.2 %copy-start.2 = (s32[128]{0:T(128)}, s32[128]{0:T(128)S(1)}, u32[]{:S(2)}) copy-start(s32[128]{0:T(128)S(1)} %get-tuple-element.36) | copy-start | bytes 1540
  179.3 0.6 copy-start.6
  271.7 0.7 copy-start.7
  271.7 1.4 copy-start.3
  271.7 1.4 copy-start.4
  271.7 1.4 copy-start.5
Sparse Core Ops, SparseCore 0:
  58.1 213.5 all-gather.1

commit v3 on v2

--- a/solution.py
+++ b/solution.py
@@ -17,15 +17,17 @@
 ABSORB_VMEM = 58 * 1024 * 1024
 
 
-def pack(target, labels, factors, devices):
-    items, rows, width = factors.shape
-    extra = labels.shape[1]
-    chunk = 16
-
-    def kernel(target_ref, labels_ref, factors_ref, first_ref, second_ref, held, load_sems, store_sems, label_sem):
+def pack(target, factors, devices, begin, end, boxes=(), labels=None):
+    rows, width = factors.shape[1:]
+    items, chunk, extra = end - begin, 16, 16
+    labelled = [] if labels is None else [labels]
+
+    def kernel(target_ref, factors_ref, *refs):
+        first_ref, second_ref, held, load_sems, store_sems, label_sem = refs[-6:]
+
         def load(c):
-            part = pl.ds(c * chunk, chunk)
-            return pltpu.make_async_copy(factors_ref.at[part], held.at[part], load_sems.at[c])
+            part = factors_ref.at[pl.ds(begin + c * chunk, chunk)]
+            return pltpu.make_async_copy(part, held.at[pl.ds(c * chunk, chunk)], load_sems.at[c])
 
         def to_first(k, place):
             return pltpu.make_async_copy(held.at[k], first_ref.at[place, pl.ds(0, rows)], store_sems.at[k])
@@ -37,8 +39,9 @@
         def _(c):
             load(c).start()
 
-        tail = pltpu.make_async_copy(labels_ref, first_ref.at[:, pl.ds(rows, extra)], label_sem)
-        tail.start()
+        if labelled:
+            tail = pltpu.make_async_copy(refs[0], first_ref.at[:, pl.ds(rows, extra)], label_sem)
+            tail.start()
 
         @pl.loop(0, items // chunk)
         def _(c):
@@ -47,7 +50,7 @@
             @pl.loop(0, chunk)
             def _(i):
                 k = c * chunk + i
-                place = target_ref[k]
+                place = target_ref[begin + k]
 
                 @pl.when(place < devices)
                 def _():
@@ -57,22 +60,26 @@
                 def _():
                     to_second(k, place - devices).start()
 
-        tail.wait()
+        if labelled:
+            tail.wait()
 
         @pl.loop(0, items)
         def _(k):
             to_second(k, 0).wait()
 
-    size = items * rows * width * 2
     hbm = pl.BlockSpec(memory_space=pltpu.HBM)
+    before = 2 + len(labelled)
     return pl.pallas_call(
         kernel,
         out_shape=(
             pltpu.HBM((devices, rows + extra, width), factors.dtype),
             pltpu.HBM((devices, rows, width), factors.dtype),
         ),
-        in_specs=[pl.BlockSpec(memory_space=pltpu.SMEM), pl.BlockSpec(memory_space=pltpu.VMEM), hbm],
+        in_specs=[pl.BlockSpec(memory_space=pltpu.SMEM), hbm]
+        + [pl.BlockSpec(memory_space=pltpu.VMEM)] * len(labelled)
+        + [hbm] * len(boxes),
         out_specs=[hbm] * 2,
+        input_output_aliases={before + i: i for i in range(len(boxes))},
         scratch_shapes=[
             pltpu.VMEM((items, rows, width), factors.dtype),
             pltpu.SemaphoreType.DMA((items // chunk,)),
@@ -80,9 +87,9 @@
             pltpu.SemaphoreType.DMA,
         ],
         compiler_params=pltpu.CompilerParams(vmem_limit_bytes=PACK_VMEM),
-        cost_estimate=pl.CostEstimate(flops=0, bytes_accessed=2 * size, transcendentals=0),
+        cost_estimate=pl.CostEstimate(flops=0, bytes_accessed=items * rows * width * 4, transcendentals=0),
         name="pack",
-    )(target, labels, factors)
+    )(target, factors, *labelled, *boxes)
 
 
 def plan(tags, tiles):
@@ -107,49 +114,21 @@
     return entry, jnp.minimum(group_tile, tiles - 1), end[tiles - 1 :]
 
 
-def absorb(tags, inbox, base, update=()):
+def absorb(tags, inbox, base):
     slots, _, width = inbox.shape
     tiles, rows, _ = base.shape
     half = width // 2
-    quarter = tiles // 4
-
-    def kernel(entry_ref, tile_ref, count_ref, inbox_ref, base_ref, *refs):
-        if update:
-            front_ref, weights_ref, out_ref, held, total, sems, front = refs
-        else:
-            out_ref, held, total, sems = refs
+
+    def kernel(entry_ref, tile_ref, count_ref, inbox_ref, base_ref, out_ref, held, total, sems):
         lane = lax.broadcasted_iota(jnp.int32, (16, width), 1)
-
-        def load(q, kind):
-            part = pl.ds(q * quarter, quarter)
-            if kind:
-                return pltpu.make_async_copy(front_ref.at[part], front.at[part], sems.at[4 + q])
-            return pltpu.make_async_copy(base_ref.at[part], total.at[part], sems.at[q])
-
-        for q in range(4):
-            load(q, 0).start()
-            if update:
-                load(q, 1).start()
-        items = pltpu.make_async_copy(inbox_ref.at[:, pl.ds(0, rows)], held, sems.at[8])
-        items.start()
-
-        for q in range(4):
-            load(q, 0).wait()
-            if update:
-                load(q, 1).wait()
-
-                @pl.loop(0, quarter // 2)
-                def _(t):
-                    pair = pl.ds(q * quarter + 2 * t, 2)
-                    product = jnp.dot(
-                        front[pair].reshape(2 * rows, rows),
-                        weights_ref[...],
-                        precision=HIGHEST,
-                        preferred_element_type=jnp.float32,
-                    )
-                    total[pair] -= product.reshape(2, rows, rows)
-
-        items.wait()
+        copies = [
+            pltpu.make_async_copy(inbox_ref.at[:, pl.ds(0, rows)], held, sems.at[0]),
+            pltpu.make_async_copy(base_ref, total, sems.at[1]),
+        ]
+        for copy in copies:
+            copy.start()
+        for copy in copies:
+            copy.wait()
 
         def product(group):
             first = entry_ref[GROUP * group]
@@ -181,20 +160,22 @@
             for u in range(UNROLL):
                 total[tile_ref[step * UNROLL + u]] += products[u]
 
-        result = pltpu.make_async_copy(total, out_ref, sems.at[9])
+        result = pltpu.make_async_copy(total, out_ref, sems.at[2])
         result.start()
         result.wait()
 
-    smem, vmem = pl.BlockSpec(memory_space=pltpu.SMEM), pl.BlockSpec(memory_space=pltpu.VMEM)
+    smem = pl.BlockSpec(memory_space=pltpu.SMEM)
     hbm = pl.BlockSpec(memory_space=pltpu.HBM)
-    tiled = pltpu.VMEM(base.shape, base.dtype)
     return pl.pallas_call(
         kernel,
         out_shape=pltpu.HBM(base.shape, base.dtype),
-        in_specs=[smem] * 3 + [hbm] * 2 + [hbm, vmem][: len(update)],
+        in_specs=[smem] * 3 + [hbm] * 2,
         out_specs=hbm,
-        scratch_shapes=[pltpu.VMEM((slots, rows, width), inbox.dtype), tiled, pltpu.SemaphoreType.DMA((10,))]
-        + [tiled][: len(update)],
+        scratch_shapes=[
+            pltpu.VMEM((slots, rows, width), inbox.dtype),
+            pltpu.VMEM(base.shape, base.dtype),
+            pltpu.SemaphoreType.DMA((3,)),
+        ],
         compiler_params=pltpu.CompilerParams(vmem_limit_bytes=ABSORB_VMEM),
         cost_estimate=pl.CostEstimate(
             flops=2 * slots * rows * rows * half,
@@ -202,23 +183,58 @@
             transcendentals=0,
         ),
         name="absorb",
-    )(*plan(tags, tiles), inbox, base, *update)
-
-
-def hold(array):
-    def kernel(array_ref, out_ref):
-        pass
+    )(*plan(tags, tiles), inbox, base)
+
+
+def subtract(base, front, weights):
+    tiles, rows, depth = front.shape
+    parts = 8
+    size = tiles // parts
+
+    def kernel(base_ref, front_ref, weights_ref, out_ref, total, held, sems):
+        def copy(q, kind):
+            part = pl.ds(q * size, size)
+            ends = [(base_ref, total), (front_ref, held), (total, out_ref)][kind]
+            return pltpu.make_async_copy(ends[0].at[part], ends[1].at[part], sems.at[kind, q])
+
+        @pl.loop(0, parts)
+        def _(q):
+            copy(q, 0).start()
+            copy(q, 1).start()
+
+        @pl.loop(0, parts)
+        def _(q):
+            copy(q, 0).wait()
+            copy(q, 1).wait()
+            part = pl.ds(q * size, size)
+            product = jnp.dot(
+                held[part].reshape(size * rows, depth),
+                weights_ref[...],
+                precision=HIGHEST,
+                preferred_element_type=jnp.float32,
+            )
+            total[part] -= product.reshape(size, rows, -1)
+            copy(q, 2).start()
+
+        @pl.loop(0, parts)
+        def _(q):
+            copy(q, 2).wait()
 
     hbm = pl.BlockSpec(memory_space=pltpu.HBM)
     return pl.pallas_call(
         kernel,
-        out_shape=pltpu.HBM(array.shape, array.dtype),
-        in_specs=[hbm],
+        out_shape=pltpu.HBM(base.shape, base.dtype),
+        in_specs=[hbm, hbm, pl.BlockSpec(memory_space=pltpu.VMEM)],
         out_specs=hbm,
-        input_output_aliases={0: 0},
-        cost_estimate=pl.CostEstimate(flops=SCHEDULED_FLOPS, bytes_accessed=0, transcendentals=0),
-        name="hold",
-    )(array)
+        scratch_shapes=[
+            pltpu.VMEM(base.shape, base.dtype),
+            pltpu.VMEM(front.shape, front.dtype),
+            pltpu.SemaphoreType.DMA((3, parts)),
+        ],
+        compiler_params=pltpu.CompilerParams(vmem_limit_bytes=ABSORB_VMEM),
+        cost_estimate=pl.CostEstimate(flops=SCHEDULED_FLOPS, bytes_accessed=3 * base.size * 4, transcendentals=0),
+        name="subtract",
+    )(base, front, weights)
 
 
 def inverse_factor(block):
@@ -258,7 +274,7 @@
     facts = jnp.max(jnp.where(lands[None], facts[:, None, :], 0), axis=2).reshape(2, 2, devices)
     facts = facts.transpose(2, 1, 0).reshape(devices, 1, 4).astype(factors.dtype)
     labels = jnp.pad(facts, ((0, 0), (0, 15), (0, factors.shape[2] - 4)))
-    first_out, second_out = pack(target, labels, factors, devices)
+    boxes = pack(target, factors, devices, 0, items // 2)
 
     def spread(value, steps):
         return sum([lax.ppermute(value, ALL, pairs) for pairs in steps])
@@ -279,9 +295,11 @@
     along_x = [[(number(0, 0, z, y), number(x, 0, z, y)) for z in four for y in four] for x in (1, 2, 3)]
     swap = [[(number(x, c, z, y), number(x, 1 - c, z, y)) for x in four for c in (0, 1) for z in four for y in four]]
     held = jnp.where((me == 0) | ((x == 0) & (core == 1)), panel, spread(panel, first_hop))
-    held, first_out, second_out = lax.optimization_barrier((held, first_out, second_out))
-    for steps in (along_z, along_x):
-        held = held + spread(held, steps)
+    held, boxes = lax.optimization_barrier((held, boxes))
+    held = held + spread(held, along_z)
+    boxes = pack(target, factors, devices, items // 2, items, boxes, labels)
+    held, (first_out, second_out) = lax.optimization_barrier((held, boxes))
+    held = held + spread(held, along_x)
     other = spread(held, swap)
     diagonal, columns_panel = jnp.where(core == 0, held, other), jnp.where(core == 0, other, held)
 
@@ -300,8 +318,8 @@
     weights = jnp.dot(inverse.T, columns.T, precision=HIGHEST)
     tiled = (cols_devs, tile, tile)
     total = absorb(first_tags, first_in, trailing.reshape(tiled))
-    front, total = lax.optimization_barrier((front.reshape(tiled), total))
-    total = absorb(second_tags, second_in, total, (hold(front), weights))
+    total = subtract(total, front.reshape(tiled), weights)
+    total = absorb(second_tags, second_in, total)
     return (total.reshape(cols_devs * tile, tile), lower)
 
 

time: 311 us -> 304 us (0.977)
  waiting for transfers between devices: 170 us -> 156 us
  Pallas kernels: 36.8 us -> 43 us
    all_to_all x1, waiting for transfers between devices: 14.7 us -> 6.02 us  [shards(): lax.all_to_all(second_out, ALL, split_axis=0, concat_axis=0, tiled=True)]
    pallas_call x1, Pallas kernels: 0.01 us -> 7.87 us  [subtract(): pl.pallas_call(kernel, out_shape=pltpu.HBM(base.shape, base.dtype), in_sp...]
    ppermute x10, waiting for transfers between devices: 18 us -> 11.6 us  [spread(): return sum([lax.ppermute(value, ALL, pairs) for pairs in steps])]
    pallas_call x1 -> x2, Pallas kernels: 8.77 us -> 9.72 us  [pack(): pl.pallas_call(kernel, out_shape=(pltpu.HBM((devices, rows + extra, width...]
  transfers between devices with their start and end apart: 13 -> 13, of which waited for: 5 -> 5; matrix products, arithmetic and copies ran while one was open for 20% -> 20% of each run, Pallas kernels for 7% -> 10%
where the time goes in v3:
time: 304 us; the launch traced here: 302 us
  waiting for transfers between devices  156 us (51%)
  other arithmetic  54.3 us (18%)
  Pallas kernels  43 us (14%)
  starting transfers between devices  25.1 us (8%)
  between operations  14.6 us (5%)
  local copies, waits for them, and re-layouts  5.1 us (2%)
  matrix products  3.87 us (1%)
    all_gather x1, waiting for transfers between devices, shards(): front = lax.all_gather(panel, COL, axis=0, tiled=True)  76.8 us
    all_to_all x1, waiting for transfers between devices, shards(): lax.all_to_all(first_out, ALL, split_axis=0, concat_axis=0, tiled=True)  61 us
    pallas_call x2, Pallas kernels, absorb(): pl.pallas_call(kernel, out_shape=pltpu.HBM(base.shape, base.dtype), in_sp...  25.4 us
    another operation x6, other arithmetic, invert(): factor = jnp.linalg.cholesky(part)  24.8 us
    another operation x4, other arithmetic, invert(): return lax.linalg.triangular_solve(factor, eye, left_side=True, lower=True)  21.1 us
    ppermute x10, waiting for transfers between devices, spread(): return sum([lax.ppermute(value, ALL, pairs) for pairs in steps])  11.6 us
    pallas_call x2, Pallas kernels, pack(): pl.pallas_call(kernel, out_shape=(pltpu.HBM((devices, rows + extra, width...  9.72 us
    all_to_all x1, starting transfers between devices, shards(): lax.all_to_all(first_out, ALL, split_axis=0, concat_axis=0, tiled=True)  9.27 us
  transfers between devices with their start and end apart: 13, of which 5 were waited for; matrix products, arithmetic and copies ran while one was open for 20% of the time, Pallas kernels for 10%

profile of v3, /device:TPU:102, one launch (start us, length us, event | category | flops | bytes accessed | tf_op | source)
XLA Modules:
  0.0 302.0 jit_solution(15925258964347919917)
XLA Ops:
  7.2 1.1 copy.37
  10.3 0.9 fusion.26
  11.3 1.2 select_add_fusion.target_ref
  12.4 4.6 %pack.2 = (bf16[128,272,128]{2,1,0:T(8,128)(2,1)}, bf16[128,256,128]{2,1,0:T(8,128)(2,1)}) custom-call(s32[128]{0:T(128)} %select_add_fusion.target_ref, bf16[128,256,128]{2,1,0:T(8,128)(2,1)} %factors_ref.3), custom_call_target="tpu_custom_call" | custom-call | bytes 8388608 | tf_op jit(solution)/shard_map/pack/pallas_call | solution.py:72
  19.6 0.9 pad.5.refs_0_
  20.5 5.1 %pack.3 = (bf16[128,272,128]{2,1,0:T(8,128)(2,1)}, bf16[128,256,128]{2,1,0:T(8,128)(2,1)}) custom-call(s32[128]{0:T(128)} %select_add_fusion.target_ref, bf16[128,256,128]{2,1,0:T(8,128)(2,1)} %factors_ref.3, bf16[128,16,128]{2,1,0:T(8,128)(2,1)} %pad.5.refs_0_, ...), custom_call_target="tpu_custom_call", output_to_operand_aliasing={{0}: (3, {}), {1}: (4, {})} | custom-call | bytes 8388608 | tf_op jit(solution)/shard_map/pack/pallas_call | solution.py:72
  27.1 1.3 collective-permute-start.8
  28.4 10.1 %collective-permute-done.8 = f32[256,256]{0,1:T(8,128)S(1)} collective-permute-done((f32[256,256]{0,1:T(8,128)S(1)}, f32[256,256]{0,1:T(8,128)S(1)}, u32[]{:S(2)}, u32[]{:S(2)}) %collective-permute-start.8) | collective-permute-done | bytes 262176 | tf_op jit(solution)/shard_map/ppermute | solution.py:280
  38.7 1.5 collective-permute-done.9
  40.3 9.3 %all-to-all-start = ((bf16[128,272,128]{2,1,0:T(8,128)(2,1)}), bf16[128,272,128]{2,1,0:T(8,128)(2,1)}, u32[]{:S(2)}, u32[]{:S(2)}) async-start(bf16[128,272,128]{2,1,0:T(8,128)(2,1)} %get-tuple-element.28), calls=%async_computation | async-start | bytes 17825792 | tf_op jit(solution)/shard_map/all_to_all | solution.py:307
  50.6 11.7 %cholesky.44 = f32[128,128]{1,0:T(8,128)S(1)} custom-call(f32[128,128]{1,0:T(8,128)S(1)} %fusion.21), custom_call_target="Cholesky" | custom-call | tf_op jit(solution)/shard_map/jit(cholesky)/cholesky | solution.py:245
  63.6 9.8 %custom-call.6 = f32[1,128,128]{1,2,0:T(8,128)S(1)} custom-call(f32[1,128,128]{2,1,0:T(8,128)S(1)} %fusion.4), custom_call_target="InvertDiagBlocksLowerTriangular" | custom-call | tf_op jit(solution)/shard_map/triangular_solve/custom-call.0 | solution.py:246
  74.4 11.7 %cholesky.55 = f32[128,128]{1,0:T(8,128)S(1)} custom-call(f32[128,128]{1,0:T(8,128)S(1)} %fusion.18), custom_call_target="Cholesky" | custom-call | tf_op jit(solution)/shard_map/jit(cholesky)/cholesky | solution.py:245
  87.4 10.0 %custom-call.7 = f32[1,128,128]{1,2,0:T(8,128)S(1)} custom-call(f32[1,128,128]{2,1,0:T(8,128)S(1)} %fusion.5), custom_call_target="InvertDiagBlocksLowerTriangular" | custom-call | tf_op jit(solution)/shard_map/triangular_solve/custom-call.0 | solution.py:246
  98.8 0.8 copy.46
  100.2 1.3 fusion.39.weights_ref
  101.5 61.0 %all-to-all-done.inbox_ref = bf16[128,272,128]{2,1,0:T(8,128)(2,1)} async-done(((bf16[128,272,128]{2,1,0:T(8,128)(2,1)}), bf16[128,272,128]{2,1,0:T(8,128)(2,1)}, u32[]{:S(2)}, u32[]{:S(2)}) %all-to-all-start) | async-done | bytes 8912928 | tf_op jit(solution)/shard_map/all_to_all | solution.py:307
  162.5 8.8 %all-to-all-start.1 = ((bf16[128,256,128]{2,1,0:T(8,128)(2,1)}), bf16[128,256,128]{2,1,0:T(8,128)(2,1)}, u32[]{:S(2)}, u32[]{:S(2)}) async-start(bf16[128,256,128]{2,1,0:T(8,128)(2,1)} %get-tuple-element.31), calls=%async_computation.1 | async-start | bytes 16777216 | tf_op jit(solution)/shard_map/all_to_all | solution.py:311
  171.4 1.0 slice_convert_fusion
  177.0 12.4 %absorb.2.base_ref = f32[16,256,256]{2,1,0:T(8,128)} custom-call(s32[208]{0:T(256)} %select_reduce_fusion.1.entry_ref, s32[52]{0:T(128)} %broadcast_minimum_fusion.tile_ref, s32[1]{0:T(128)} %slice.49.count_ref, bf16[128,272,128]{2,1,0:T(8,128)(2,1)} %all-to-all-done.inbox_ref, f32[16,256,256]{2,1,0:T(8,128)} %bitcast.48), custom_call_target="tpu_custom_call" | custom-call | flops 1073741824 | bytes 16777216 | tf_op jit(solution)/shard_map/absorb/pallas_call | solution.py:169
  189.4 76.8 %all-gather.2.cloned.1.call-done = f32[4096,256]{1,0:T(8,128)} async-done(((f32[256,256]{1,0:T(8,128)}), f32[4096,256]{1,0:T(8,128)}) %all-gather.2.cloned.1.call-update) | async-done | bytes 4194320 | tf_op jit(solution)/shard_map/all_gather | solution.py:288
  266.2 7.9 %subtract.1.base_ref = f32[16,256,256]{2,1,0:T(8,128)} custom-call(f32[16,256,256]{2,1,0:T(8,128)} %absorb.2.base_ref, f32[16,256,256]{2,1,0:T(8,128)} %bitcast.55, f32[256,256]{1,0:T(8,128)} %fusion.39.weights_ref), custom_call_target="tpu_custom_call" | custom-call | flops 199999995904 | bytes 12582912 | tf_op jit(solution)/shard_map/subtract/pallas_call | solution.py:224
  276.1 6.0 %all-to-all-done.1.inbox_ref = bf16[128,256,128]{2,1,0:T(8,128)(2,1)} async-done(((bf16[128,256,128]{2,1,0:T(8,128)(2,1)}), bf16[128,256,128]{2,1,0:T(8,128)(2,1)}, u32[]{:S(2)}, u32[]{:S(2)}) %all-to-all-start.1) | async-done | bytes 8388640 | tf_op jit(solution)/shard_map/all_to_all | solution.py:311
  282.2 13.0 %absorb.3 = f32[16,256,256]{2,1,0:T(8,128)} custom-call(s32[208]{0:T(256)} %select_reduce_fusion.2.entry_ref, s32[52]{0:T(128)} %broadcast_minimum_fusion.1.tile_ref, s32[1]{0:T(128)} %slice.42.count_ref, bf16[128,256,128]{2,1,0:T(8,128)(2,1)} %all-to-all-done.1.inbox_ref, f32[16,256,256]{2,1,0:T(8,128)} %subtract.1.base_ref), custom_call_target="tpu_custom_call" | custom-call | flops 1073741824 | bytes 16777216 | tf_op jit(solution)/shard_map/absorb/pallas_call | solution.py:169
  (95 shorter events, 19.1 us)
Async XLA Ops:
  7.2 12.1 %copy-start.7 = (s32[128]{0:T(128)S(1)}, s32[128]{0:T(128)}, u32[]{:S(2)}) copy-start(s32[128]{0:T(128)} %param.13) | copy-start | bytes 1540
  7.2 12.1 %copy-start.6 = (s32[128]{0:T(128)S(1)}, s32[128]{0:T(128)}, u32[]{:S(2)}) copy-start(s32[128]{0:T(128)} %param.14) | copy-start | bytes 1540
  8.3 8.8 %collective-permute-start = (f32[256,256]{0,1:T(8,128)S(1)}, f32[256,256]{0,1:T(8,128)S(1)}, u32[]{:S(2)}, u32[]{:S(2)}) collective-permute-start(f32[256,256]{0,1:T(8,128)S(1)} %copy.37), channel_id=1, source_target_pairs={{0,1},{16,48},{17,49},{18,50},{19,51},{20,52},{21,53},{22,54},{23,... | collective-permute-start | bytes 786440 | tf_op jit(solution)/shard_map/ppermute | solution.py:280
  9.0 8.1 %collective-permute-start.1 = (f32[256,256]{0,1:T(8,128)S(1)}, f32[256,256]{0,1:T(8,128)S(1)}, u32[]{:S(2)}, u32[]{:S(2)}) collective-permute-start(f32[256,256]{0,1:T(8,128)S(1)} %copy.37), channel_id=1, source_target_pairs={{0,2},{16,80},{17,81},{18,82},{19,83},{20,84},{21,85},{22,86},{23,... | collective-permute-start | bytes 786440 | tf_op jit(solution)/shard_map/ppermute | solution.py:280
  9.7 7.4 %collective-permute-start.2 = (f32[256,256]{0,1:T(8,128)S(1)}, f32[256,256]{0,1:T(8,128)S(1)}, u32[]{:S(2)}, u32[]{:S(2)}) collective-permute-start(f32[256,256]{0,1:T(8,128)S(1)} %copy.37), channel_id=1, source_target_pairs={{0,3},{16,112},{17,113},{18,114},{19,115},{20,116},{21,117},{22,11... | collective-permute-start | bytes 786440 | tf_op jit(solution)/shard_map/ppermute | solution.py:280
  12.4 6.8 %copy-start.1 = (s32[128]{0:T(128)S(1)}, s32[128]{0:T(128)}, u32[]{:S(2)}) copy-start(s32[128]{0:T(128)} %select_add_fusion.target_ref) | copy-start | bytes 1540
  17.2 8.5 %collective-permute-start.3 = (f32[256,256]{0,1:T(8,128)S(1)}, f32[256,256]{0,1:T(8,128)S(1)}, u32[]{:S(2)}, u32[]{:S(2)}) collective-permute-start(f32[256,256]{0,1:T(8,128)S(1)} %add_select_fusion), channel_id=1, source_target_pairs={{0,4},{1,5},{2,6},{3,7}} | collective-permute-start | bytes 786440 | tf_op jit(solution)/shard_map/ppermute | solution.py:280
  17.8 7.8 %collective-permute-start.4 = (f32[256,256]{0,1:T(8,128)S(1)}, f32[256,256]{0,1:T(8,128)S(1)}, u32[]{:S(2)}, u32[]{:S(2)}) collective-permute-start(f32[256,256]{0,1:T(8,128)S(1)} %add_select_fusion), channel_id=1, source_target_pairs={{0,8},{1,9},{2,10},{3,11}} | collective-permute-start | bytes 786440 | tf_op jit(solution)/shard_map/ppermute | solution.py:280
  18.5 7.1 %collective-permute-start.5 = (f32[256,256]{0,1:T(8,128)S(1)}, f32[256,256]{0,1:T(8,128)S(1)}, u32[]{:S(2)}, u32[]{:S(2)}) collective-permute-start(f32[256,256]{0,1:T(8,128)S(1)} %add_select_fusion), channel_id=1, source_target_pairs={{0,12},{1,13},{2,14},{3,15}} | collective-permute-start | bytes 786440 | tf_op jit(solution)/shard_map/ppermute | solution.py:280
  25.7 2.7 collective-permute-start.6
  26.4 2.0 collective-permute-start.7
  27.1 11.4 %collective-permute-start.8 = (f32[256,256]{0,1:T(8,128)S(1)}, f32[256,256]{0,1:T(8,128)S(1)}, u32[]{:S(2)}, u32[]{:S(2)}) collective-permute-start(f32[256,256]{0,1:T(8,128)S(1)} %add_add_fusion.1), channel_id=1, source_target_pairs={{0,96},{1,97},{2,98},{3,99},{4,100},{5,101},{6,102},{7,103},{8,104... | collective-permute-start | bytes 786440 | tf_op jit(solution)/shard_map/ppermute | solution.py:280
  38.6 1.6 collective-permute-start.9
  40.3 58.1 %copy-start = (f32[256,256]{1,0:T(8,128)S(1)}, f32[256,256]{1,0:T(8,128)}, u32[]{:S(2)}) copy-start(f32[256,256]{1,0:T(8,128)} %param.9) | copy-start | bytes 786436
  40.3 122.2 %all-to-all-start = ((bf16[128,272,128]{2,1,0:T(8,128)(2,1)}), bf16[128,272,128]{2,1,0:T(8,128)(2,1)}, u32[]{:S(2)}, u32[]{:S(2)}) async-start(bf16[128,272,128]{2,1,0:T(8,128)(2,1)} %get-tuple-element.28), calls=%async_computation | async-start | bytes 17825792 | tf_op jit(solution)/shard_map/all_to_all | solution.py:307
  49.6 216.6 %all-gather.2.cloned.1.call-start = ((), (), s32[]{:S(2)}) async-start(), calls=%async_computation.2 | async-start | bytes 4456448 | tf_op jit(solution)/shard_map/all_gather | solution.py:288
  162.5 119.6 %all-to-all-start.1 = ((bf16[128,256,128]{2,1,0:T(8,128)(2,1)}), bf16[128,256,128]{2,1,0:T(8,128)(2,1)}, u32[]{:S(2)}, u32[]{:S(2)}) async-start(bf16[128,256,128]{2,1,0:T(8,128)(2,1)} %get-tuple-element.31), calls=%async_computation.1 | async-start | bytes 16777216 | tf_op jit(solution)/shard_map/all_to_all | solution.py:311
  172.7 3.1 %copy-start.2 = (s32[128]{0:T(128)}, s32[128]{0:T(128)S(1)}, u32[]{:S(2)}) copy-start(s32[128]{0:T(128)S(1)} %get-tuple-element.42) | copy-start | bytes 1540
  173.8 0.6 copy-start.8
  266.2 7.9 %copy-start.9 = (s32[16]{0:T(128)S(1)}, s32[16]{0:T(128)}, u32[]{:S(2)}) copy-start(s32[16]{0:T(128)} %copy-done.8) | copy-start | bytes 196
  266.2 8.6 %copy-start.3 = (s32[128]{0:T(128)S(1)}, s32[128]{0:T(128)}, u32[]{:S(2)}) copy-start(s32[128]{0:T(128)} %copy-done.2) | copy-start | bytes 1540
  266.2 8.6 %copy-start.4 = (s32[128]{0:T(128)S(1)}, s32[128]{0:T(128)}, u32[]{:S(2)}) copy-start(s32[128]{0:T(128)} %get-tuple-element.53) | copy-start | bytes 1540
  266.2 8.6 %copy-start.5 = (s32[128]{0:T(128)S(1)}, s32[128]{0:T(128)}, u32[]{:S(2)}) copy-start(s32[128]{0:T(128)} %get-tuple-element.51) | copy-start | bytes 1540
Sparse Core Ops, SparseCore 0:
  52.5 213.6 all-gather.1

commit v4 on v3

--- a/solution.py
+++ b/solution.py
@@ -11,6 +11,7 @@
 COL = ("z", "y")
 GROUP = 4
 UNROLL = 4
+PARTS = 8
 SCHEDULED_FLOPS = 2 * 10**11
 HIGHEST = lax.Precision.HIGHEST
 PACK_VMEM = 58 * 1024 * 1024
@@ -121,14 +122,24 @@
 
     def kernel(entry_ref, tile_ref, count_ref, inbox_ref, base_ref, out_ref, held, total, sems):
         lane = lax.broadcasted_iota(jnp.int32, (16, width), 1)
-        copies = [
-            pltpu.make_async_copy(inbox_ref.at[:, pl.ds(0, rows)], held, sems.at[0]),
-            pltpu.make_async_copy(base_ref, total, sems.at[1]),
-        ]
-        for copy in copies:
-            copy.start()
-        for copy in copies:
-            copy.wait()
+        def load(c):
+            part = pl.ds(c * (slots // PARTS), slots // PARTS)
+            return pltpu.make_async_copy(inbox_ref.at[part, pl.ds(0, rows)], held.at[part], sems.at[0, c])
+
+        def sums(c, kind):
+            part = pl.ds(c * (tiles // PARTS), tiles // PARTS)
+            ends = (total, out_ref) if kind else (base_ref, total)
+            return pltpu.make_async_copy(ends[0].at[part], ends[1].at[part], sems.at[1 + kind, c])
+
+        @pl.loop(0, PARTS)
+        def _(c):
+            load(c).start()
+            sums(c, 0).start()
+
+        @pl.loop(0, PARTS)
+        def _(c):
+            load(c).wait()
+            sums(c, 0).wait()
 
         def product(group):
             first = entry_ref[GROUP * group]
@@ -160,9 +171,13 @@
             for u in range(UNROLL):
                 total[tile_ref[step * UNROLL + u]] += products[u]
 
-        result = pltpu.make_async_copy(total, out_ref, sems.at[2])
-        result.start()
-        result.wait()
+        @pl.loop(0, PARTS)
+        def _(c):
+            sums(c, 1).start()
+
+        @pl.loop(0, PARTS)
+        def _(c):
+            sums(c, 1).wait()
 
     smem = pl.BlockSpec(memory_space=pltpu.SMEM)
     hbm = pl.BlockSpec(memory_space=pltpu.HBM)
@@ -174,7 +189,7 @@
         scratch_shapes=[
             pltpu.VMEM((slots, rows, width), inbox.dtype),
             pltpu.VMEM(base.shape, base.dtype),
-            pltpu.SemaphoreType.DMA((3,)),
+            pltpu.SemaphoreType.DMA((3, PARTS)),
         ],
         compiler_params=pltpu.CompilerParams(vmem_limit_bytes=ABSORB_VMEM),
         cost_estimate=pl.CostEstimate(

time: 304 us -> 307 us (level)
  the two profiles are of different devices: /device:TPU:102 before, /device:TPU:28 now
where the time goes in v4:
time: 307 us; the launch traced here: 306 us
  waiting for transfers between devices  157 us (51%)
  other arithmetic  54.3 us (18%)
  Pallas kernels  43.9 us (14%)
  starting transfers between devices  27.6 us (9%)
  between operations  14.6 us (5%)
  local copies, waits for them, and re-layouts  5.1 us (2%)
  matrix products  3.87 us (1%)
    all_gather x1, waiting for transfers between devices, shards(): front = lax.all_gather(panel, COL, axis=0, tiled=True)  85.7 us
    all_to_all x1, waiting for transfers between devices, shards(): lax.all_to_all(first_out, ALL, split_axis=0, concat_axis=0, tiled=True)  57 us
    pallas_call x2, Pallas kernels, absorb(): pl.pallas_call(kernel, out_shape=pltpu.HBM(base.shape, base.dtype), in_sp...  26.2 us
    another operation x6, other arithmetic, invert(): factor = jnp.linalg.cholesky(part)  24.8 us
    another operation x4, other arithmetic, invert(): return lax.linalg.triangular_solve(factor, eye, left_side=True, lower=True)  21.1 us
    ppermute x10, waiting for transfers between devices, spread(): return sum([lax.ppermute(value, ALL, pairs) for pairs in steps])  13.5 us
    all_to_all x1, starting transfers between devices, shards(): lax.all_to_all(second_out, ALL, split_axis=0, concat_axis=0, tiled=True)  12.9 us
    pallas_call x2, Pallas kernels, pack(): pl.pallas_call(kernel, out_shape=(pltpu.HBM((devices, rows + extra, width...  9.79 us
  transfers between devices with their start and end apart: 13, of which 4 were waited for; matrix products, arithmetic and copies ran while one was open for 20% of the time, Pallas kernels for 10%

profile of v4, /device:TPU:28, one launch (start us, length us, event | category | flops | bytes accessed | tf_op | source)
XLA Modules:
  0.0 306.1 jit_solution(11708322354751615082)
XLA Ops:
  7.2 1.1 copy.37
  10.3 0.9 fusion.26
  11.3 1.2 select_add_fusion.target_ref
  12.4 4.7 %pack.2 = (bf16[128,272,128]{2,1,0:T(8,128)(2,1)}, bf16[128,256,128]{2,1,0:T(8,128)(2,1)}) custom-call(s32[128]{0:T(128)} %select_add_fusion.target_ref, bf16[128,256,128]{2,1,0:T(8,128)(2,1)} %factors_ref.3), custom_call_target="tpu_custom_call" | custom-call | bytes 8388608 | tf_op jit(solution)/shard_map/pack/pallas_call | solution.py:73
  19.7 0.9 pad.5.refs_0_
  20.6 5.1 %pack.3 = (bf16[128,272,128]{2,1,0:T(8,128)(2,1)}, bf16[128,256,128]{2,1,0:T(8,128)(2,1)}) custom-call(s32[128]{0:T(128)} %select_add_fusion.target_ref, bf16[128,256,128]{2,1,0:T(8,128)(2,1)} %factors_ref.3, bf16[128,16,128]{2,1,0:T(8,128)(2,1)} %pad.5.refs_0_, ...), custom_call_target="tpu_custom_call", output_to_operand_aliasing={{0}: (3, {}), {1}: (4, {})} | custom-call | bytes 8388608 | tf_op jit(solution)/shard_map/pack/pallas_call | solution.py:73
  26.5 1.3 collective-permute-start.7
  28.5 12.0 %collective-permute-done.7 = f32[256,256]{0,1:T(8,128)S(1)} collective-permute-done((f32[256,256]{0,1:T(8,128)S(1)}, f32[256,256]{0,1:T(8,128)S(1)}, u32[]{:S(2)}, u32[]{:S(2)}) %collective-permute-start.7) | collective-permute-done | bytes 262176 | tf_op jit(solution)/shard_map/ppermute | solution.py:295
  40.7 1.5 collective-permute-done.9
  42.2 7.7 %all-to-all-start = ((bf16[128,272,128]{2,1,0:T(8,128)(2,1)}), bf16[128,272,128]{2,1,0:T(8,128)(2,1)}, u32[]{:S(2)}, u32[]{:S(2)}) async-start(bf16[128,272,128]{2,1,0:T(8,128)(2,1)} %get-tuple-element.28), calls=%async_computation | async-start | bytes 17825792 | tf_op jit(solution)/shard_map/all_to_all | solution.py:322
  51.0 11.7 %cholesky.44 = f32[128,128]{1,0:T(8,128)S(1)} custom-call(f32[128,128]{1,0:T(8,128)S(1)} %fusion.21), custom_call_target="Cholesky" | custom-call | tf_op jit(solution)/shard_map/jit(cholesky)/cholesky | solution.py:260
  64.0 9.8 %custom-call.6 = f32[1,128,128]{1,2,0:T(8,128)S(1)} custom-call(f32[1,128,128]{2,1,0:T(8,128)S(1)} %fusion.4), custom_call_target="InvertDiagBlocksLowerTriangular" | custom-call | tf_op jit(solution)/shard_map/triangular_solve/custom-call.0 | solution.py:261
  74.8 11.7 %cholesky.55 = f32[128,128]{1,0:T(8,128)S(1)} custom-call(f32[128,128]{1,0:T(8,128)S(1)} %fusion.18), custom_call_target="Cholesky" | custom-call | tf_op jit(solution)/shard_map/jit(cholesky)/cholesky | solution.py:260
  87.9 10.0 %custom-call.7 = f32[1,128,128]{1,2,0:T(8,128)S(1)} custom-call(f32[1,128,128]{2,1,0:T(8,128)S(1)} %fusion.5), custom_call_target="InvertDiagBlocksLowerTriangular" | custom-call | tf_op jit(solution)/shard_map/triangular_solve/custom-call.0 | solution.py:261
  99.2 0.8 copy.46
  100.6 1.3 fusion.39.weights_ref
  101.9 57.0 %all-to-all-done.inbox_ref = bf16[128,272,128]{2,1,0:T(8,128)(2,1)} async-done(((bf16[128,272,128]{2,1,0:T(8,128)(2,1)}), bf16[128,272,128]{2,1,0:T(8,128)(2,1)}, u32[]{:S(2)}, u32[]{:S(2)}) %all-to-all-start) | async-done | bytes 8912928 | tf_op jit(solution)/shard_map/all_to_all | solution.py:322
  158.9 12.9 %all-to-all-start.1 = ((bf16[128,256,128]{2,1,0:T(8,128)(2,1)}), bf16[128,256,128]{2,1,0:T(8,128)(2,1)}, u32[]{:S(2)}, u32[]{:S(2)}) async-start(bf16[128,256,128]{2,1,0:T(8,128)(2,1)} %get-tuple-element.31), calls=%async_computation.1 | async-start | bytes 16777216 | tf_op jit(solution)/shard_map/all_to_all | solution.py:326
  171.8 1.0 slice_convert_fusion
  175.4 0.8 convert_reduce_fusion
  177.4 13.1 %absorb.2.base_ref = f32[16,256,256]{2,1,0:T(8,128)} custom-call(s32[208]{0:T(256)} %select_reduce_fusion.1.entry_ref, s32[52]{0:T(128)} %broadcast_minimum_fusion.tile_ref, s32[1]{0:T(128)} %slice.49.count_ref, bf16[128,272,128]{2,1,0:T(8,128)(2,1)} %all-to-all-done.inbox_ref, f32[16,256,256]{2,1,0:T(8,128)} %bitcast.48), custom_call_target="tpu_custom_call" | custom-call | flops 1073741824 | bytes 16777216 | tf_op jit(solution)/shard_map/absorb/pallas_call | solution.py:184
  190.4 85.7 %all-gather.2.cloned.1.call-done = f32[4096,256]{1,0:T(8,128)} async-done(((f32[256,256]{1,0:T(8,128)}), f32[4096,256]{1,0:T(8,128)}) %all-gather.2.cloned.1.call-update) | async-done | bytes 4194320 | tf_op jit(solution)/shard_map/all_gather | solution.py:303
  276.2 7.9 %subtract.1.base_ref = f32[16,256,256]{2,1,0:T(8,128)} custom-call(f32[16,256,256]{2,1,0:T(8,128)} %absorb.2.base_ref, f32[16,256,256]{2,1,0:T(8,128)} %bitcast.55, f32[256,256]{1,0:T(8,128)} %fusion.39.weights_ref), custom_call_target="tpu_custom_call" | custom-call | flops 199999995904 | bytes 12582912 | tf_op jit(solution)/shard_map/subtract/pallas_call | solution.py:239
  286.1 13.2 %absorb.3 = f32[16,256,256]{2,1,0:T(8,128)} custom-call(s32[208]{0:T(256)} %select_reduce_fusion.2.entry_ref, s32[52]{0:T(128)} %broadcast_minimum_fusion.1.tile_ref, s32[1]{0:T(128)} %slice.42.count_ref, bf16[128,256,128]{2,1,0:T(8,128)(2,1)} %all-to-all-done.1.inbox_ref, f32[16,256,256]{2,1,0:T(8,128)} %subtract.1.base_ref), custom_call_target="tpu_custom_call" | custom-call | flops 1073741824 | bytes 16777216 | tf_op jit(solution)/shard_map/absorb/pallas_call | solution.py:184
  (95 shorter events, 18.3 us)
Async XLA Ops:
  7.2 12.2 %copy-start.7 = (s32[128]{0:T(128)S(1)}, s32[128]{0:T(128)}, u32[]{:S(2)}) copy-start(s32[128]{0:T(128)} %param.13) | copy-start | bytes 1540
  7.2 12.2 %copy-start.6 = (s32[128]{0:T(128)S(1)}, s32[128]{0:T(128)}, u32[]{:S(2)}) copy-start(s32[128]{0:T(128)} %param.14) | copy-start | bytes 1540
  8.3 8.8 %collective-permute-start = (f32[256,256]{0,1:T(8,128)S(1)}, f32[256,256]{0,1:T(8,128)S(1)}, u32[]{:S(2)}, u32[]{:S(2)}) collective-permute-start(f32[256,256]{0,1:T(8,128)S(1)} %copy.37), channel_id=1, source_target_pairs={{0,1},{16,48},{17,49},{18,50},{19,51},{20,52},{21,53},{22,54},{23,... | collective-permute-start | bytes 786440 | tf_op jit(solution)/shard_map/ppermute | solution.py:295
  9.0 8.2 %collective-permute-start.1 = (f32[256,256]{0,1:T(8,128)S(1)}, f32[256,256]{0,1:T(8,128)S(1)}, u32[]{:S(2)}, u32[]{:S(2)}) collective-permute-start(f32[256,256]{0,1:T(8,128)S(1)} %copy.37), channel_id=1, source_target_pairs={{0,2},{16,80},{17,81},{18,82},{19,83},{20,84},{21,85},{22,86},{23,... | collective-permute-start | bytes 786440 | tf_op jit(solution)/shard_map/ppermute | solution.py:295
  9.7 7.5 %collective-permute-start.2 = (f32[256,256]{0,1:T(8,128)S(1)}, f32[256,256]{0,1:T(8,128)S(1)}, u32[]{:S(2)}, u32[]{:S(2)}) collective-permute-start(f32[256,256]{0,1:T(8,128)S(1)} %copy.37), channel_id=1, source_target_pairs={{0,3},{16,112},{17,113},{18,114},{19,115},{20,116},{21,117},{22,11... | collective-permute-start | bytes 786440 | tf_op jit(solution)/shard_map/ppermute | solution.py:295
  12.4 6.9 %copy-start.1 = (s32[128]{0:T(128)S(1)}, s32[128]{0:T(128)}, u32[]{:S(2)}) copy-start(s32[128]{0:T(128)} %select_add_fusion.target_ref) | copy-start | bytes 1540
  17.2 8.5 %collective-permute-start.3 = (f32[256,256]{0,1:T(8,128)S(1)}, f32[256,256]{0,1:T(8,128)S(1)}, u32[]{:S(2)}, u32[]{:S(2)}) collective-permute-start(f32[256,256]{0,1:T(8,128)S(1)} %add_select_fusion), channel_id=1, source_target_pairs={{0,4},{1,5},{2,6},{3,7}} | collective-permute-start | bytes 786440 | tf_op jit(solution)/shard_map/ppermute | solution.py:295
  17.9 7.8 %collective-permute-start.4 = (f32[256,256]{0,1:T(8,128)S(1)}, f32[256,256]{0,1:T(8,128)S(1)}, u32[]{:S(2)}, u32[]{:S(2)}) collective-permute-start(f32[256,256]{0,1:T(8,128)S(1)} %add_select_fusion), channel_id=1, source_target_pairs={{0,8},{1,9},{2,10},{3,11}} | collective-permute-start | bytes 786440 | tf_op jit(solution)/shard_map/ppermute | solution.py:295
  18.6 7.1 %collective-permute-start.5 = (f32[256,256]{0,1:T(8,128)S(1)}, f32[256,256]{0,1:T(8,128)S(1)}, u32[]{:S(2)}, u32[]{:S(2)}) collective-permute-start(f32[256,256]{0,1:T(8,128)S(1)} %add_select_fusion), channel_id=1, source_target_pairs={{0,12},{1,13},{2,14},{3,15}} | collective-permute-start | bytes 786440 | tf_op jit(solution)/shard_map/ppermute | solution.py:295
  25.8 2.7 collective-permute-start.6
  26.5 14.0 %collective-permute-start.7 = (f32[256,256]{0,1:T(8,128)S(1)}, f32[256,256]{0,1:T(8,128)S(1)}, u32[]{:S(2)}, u32[]{:S(2)}) collective-permute-start(f32[256,256]{0,1:T(8,128)S(1)} %add_add_fusion.1), channel_id=1, source_target_pairs={{0,64},{1,65},{2,66},{3,67},{4,68},{5,69},{6,70},{7,71},{8,72},{9,... | collective-permute-start | bytes 786440 | tf_op jit(solution)/shard_map/ppermute | solution.py:295
  27.8 12.7 %collective-permute-start.8 = (f32[256,256]{0,1:T(8,128)S(1)}, f32[256,256]{0,1:T(8,128)S(1)}, u32[]{:S(2)}, u32[]{:S(2)}) collective-permute-start(f32[256,256]{0,1:T(8,128)S(1)} %add_add_fusion.1), channel_id=1, source_target_pairs={{0,96},{1,97},{2,98},{3,99},{4,100},{5,101},{6,102},{7,103},{8,104... | collective-permute-start | bytes 786440 | tf_op jit(solution)/shard_map/ppermute | solution.py:295
  40.6 1.6 collective-permute-start.9
  42.2 56.5 %copy-start = (f32[256,256]{1,0:T(8,128)S(1)}, f32[256,256]{1,0:T(8,128)}, u32[]{:S(2)}) copy-start(f32[256,256]{1,0:T(8,128)} %param.9) | copy-start | bytes 786436
  42.2 116.7 %all-to-all-start = ((bf16[128,272,128]{2,1,0:T(8,128)(2,1)}), bf16[128,272,128]{2,1,0:T(8,128)(2,1)}, u32[]{:S(2)}, u32[]{:S(2)}) async-start(bf16[128,272,128]{2,1,0:T(8,128)(2,1)} %get-tuple-element.28), calls=%async_computation | async-start | bytes 17825792 | tf_op jit(solution)/shard_map/all_to_all | solution.py:322
  50.0 226.2 %all-gather.2.cloned.1.call-start = ((), (), s32[]{:S(2)}) async-start(), calls=%async_computation.2 | async-start | bytes 4456448 | tf_op jit(solution)/shard_map/all_gather | solution.py:303
  158.9 127.2 %all-to-all-start.1 = ((bf16[128,256,128]{2,1,0:T(8,128)(2,1)}), bf16[128,256,128]{2,1,0:T(8,128)(2,1)}, u32[]{:S(2)}, u32[]{:S(2)}) async-start(bf16[128,256,128]{2,1,0:T(8,128)(2,1)} %get-tuple-element.31), calls=%async_computation.1 | async-start | bytes 16777216 | tf_op jit(solution)/shard_map/all_to_all | solution.py:326
  173.1 3.1 %copy-start.2 = (s32[128]{0:T(128)}, s32[128]{0:T(128)S(1)}, u32[]{:S(2)}) copy-start(s32[128]{0:T(128)S(1)} %get-tuple-element.42) | copy-start | bytes 1540
  174.2 0.6 copy-start.8
  276.2 7.9 %copy-start.9 = (s32[16]{0:T(128)S(1)}, s32[16]{0:T(128)}, u32[]{:S(2)}) copy-start(s32[16]{0:T(128)} %copy-done.8) | copy-start | bytes 196
  276.2 8.6 %copy-start.3 = (s32[128]{0:T(128)S(1)}, s32[128]{0:T(128)}, u32[]{:S(2)}) copy-start(s32[128]{0:T(128)} %copy-done.2) | copy-start | bytes 1540
  276.2 8.6 %copy-start.4 = (s32[128]{0:T(128)S(1)}, s32[128]{0:T(128)}, u32[]{:S(2)}) copy-start(s32[128]{0:T(128)} %get-tuple-element.53) | copy-start | bytes 1540
  276.2 8.6 %copy-start.5 = (s32[128]{0:T(128)S(1)}, s32[128]{0:T(128)}, u32[]{:S(2)}) copy-start(s32[128]{0:T(128)} %get-tuple-element.51) | copy-start | bytes 1540
Sparse Core Ops, SparseCore 0:
  53.0 223.1 all-gather.1
